TPU v7x, 128 devices: a whole 4x4x4 slice. The times are simulated.
128 devices in a mesh: dom: 128 (over x, z, y, core).
Axes of the slice: x: 4, y: 4, z: 4, core: 2. Of those that a mesh axis runs over, the one named last changes fastest.
Arguments:
- feats: bfloat16 [131072, 512], P('dom'), may hold values from -6 to 6
- stale_feats: bfloat16 [131072, 512], P('dom'), may hold values from -6 to 6
- grad_out: bfloat16 [131072, 512], P('dom'), may hold values from -6 to 6
- stale_bgrad: bfloat16 [131072, 512], P('dom'), may hold values from -6 to 6
- w_self: bfloat16 [512, 512], replicated, may hold values from -0.25 to 0.25
- w_neigh: bfloat16 [512, 512], replicated, may hold values from -0.25 to 0.25
- adj_tiles: bfloat16 [1024, 16, 128, 128], P('dom'), may hold values from -0.1875 to 0.1875
- tile_source_rows: int32 [1024, 16], P('dom'), may hold values from 0 to 23
- tile_cnt: int32 [1024], P('dom'), may hold values from 1 to 16, as said below
- send_idx: int32 [16384, 16], P('dom'), may hold values from 0 to 1023
- send_cnt: int32 [128, 128], P('dom'), may hold values from 1 to 16, as said below
Outputs:
- activated: bfloat16 [131072, 512], P('dom')
- grad_feats: bfloat16 [131072, 512], P('dom')
- next_bgrad: bfloat16 [131072, 512], P('dom')
- grad_w_self: float32 [512, 512], replicated
- grad_w_neigh: float32 [512, 512], replicated
Inputs may be any that keep to these rules, and one draw needn't show every extreme that they name: `tile_cnt`: each destination tile uses 1 to 16 slots; some destination tile uses all 16 in every draw. `send_cnt`: each pair of partitions uses 1 to 16 slots; every partition fills all 16 slots to some peer in every draw.
All inputs are finite; a program needn't handle non-finite values.
Results may differ from a plain program's by a relative error of at most 0.0064.
Values may be sent and summed in bfloat16 or wider, within the bound.
No kernel may reach another device: no remote copies, remote signals or barrier semaphores. Data moves between devices by JAX's collectives and lax.ppermute only.
A program may use at most 128 MiB of HBM per device.

v0:
```python
import functools

import jax
import jax.numpy as jnp
from jax import lax
from jax.experimental import pallas as pl
from jax.experimental.pallas import tpu as pltpu
from jax.sharding import PartitionSpec as P

BF16 = jnp.bfloat16
F32 = jnp.float32
LANES = 128
MIB = 1 << 20
GELU_SLOPE = 0.7978845608028654
GELU_CUBIC = 0.044715


def dot(a, b):
    return jnp.dot(a, b, preferred_element_type=F32)


def whole(shape):
    return pl.BlockSpec(shape, lambda *_: (0,) * len(shape))


def scalars():
    return pl.BlockSpec(memory_space=pltpu.SMEM)


def anywhere():
    return pl.BlockSpec(memory_space=pl.ANY)


def in_vmem():
    return pl.BlockSpec(memory_space=pltpu.VMEM)


SMALL_PARAMS = pltpu.CompilerParams(vmem_limit_bytes=16 * MIB)
PARAMS = pltpu.CompilerParams(vmem_limit_bytes=56 * MIB)
LAYER_PARAMS = pltpu.CompilerParams(vmem_limit_bytes=48 * MIB)
BACK_PARAMS = pltpu.CompilerParams(vmem_limit_bytes=56 * MIB)
LAY_PARAMS = pltpu.CompilerParams(vmem_limit_bytes=52 * MIB)


def cost(macs, moved):
    return pl.CostEstimate(flops=2 * macs, bytes_accessed=moved, transcendentals=0)


def live_slots(idx_ref, cnt_ref):
    live = lax.broadcasted_iota(jnp.int32, idx_ref.shape, 0) < cnt_ref[...]
    return jnp.where(live, idx_ref[...], -1)


def one_hot(idx, nodes, start, count):
    node_ids = lax.broadcasted_iota(jnp.int32, (idx.shape[0], nodes), 1)
    picks = [
        jnp.where(idx[:, t : t + 1] == node_ids, 1.0, 0.0).astype(BF16)
        for t in range(start, start + count)
    ]
    return jnp.concatenate(picks, axis=0)


def gather_kernel(idx_ref, cnt_ref, rows_ref, out_ref, rows, buf, sem, sems, *, groups):
    slots, peers = idx_ref.shape
    nodes, width = rows.shape
    load = pltpu.make_async_copy(rows_ref, rows, sem)
    load.start()
    idx = live_slots(idx_ref, cnt_ref)
    per = peers // groups
    copies = []
    for g in range(groups):
        picks = one_hot(idx, nodes, g * per, per)
        if g == 0:
            load.wait()
        span = pl.ds(g * per, per)
        buf[span] = dot(picks, rows[...]).astype(BF16).reshape(per, slots, width)
        copy = pltpu.make_async_copy(buf.at[span], out_ref.at[span], sems.at[g])
        copy.start()
        copies.append(copy)
    for copy in copies:
        copy.wait()


def gather(slot_rows, send_cnt, stale_feats, groups=8):
    slots, peers = slot_rows.shape
    nodes, width = stale_feats.shape
    return pl.pallas_call(
        functools.partial(gather_kernel, groups=groups),
        out_shape=jax.ShapeDtypeStruct((peers, slots, width), BF16),
        in_specs=[in_vmem()] * 2 + [anywhere()],
        out_specs=anywhere(),
        scratch_shapes=[
            pltpu.VMEM((nodes, width), BF16),
            pltpu.VMEM((peers, slots, width), BF16),
            pltpu.SemaphoreType.DMA,
            pltpu.SemaphoreType.DMA((groups,)),
        ],
        compiler_params=PARAMS,
        cost_estimate=cost(peers * slots * nodes * width, 3 * MIB),
        name="gather_rows",
    )(slot_rows, send_cnt, stale_feats)


def combine_kernel(
    src_ref, cnt_ref, adj_ref, feats_ref, ws_ref, wn_ref,
    cb_ref, cbt_ref, cot_ref, self_ref, own_ref, wst_ref, wnt_ref,
    acc,
):
    i = pl.program_id(0)
    tiles, rows = acc.shape[0], acc.shape[1]
    own_tiles = feats_ref.shape[0] // rows
    acc[...] = jnp.zeros_like(acc)

    @pl.when(i == 0)
    def _():
        wst_ref[...] = ws_ref[...].T
        wnt_ref[...] = wn_ref[...].T

    @pl.loop(0, cnt_ref[i])
    def _(j):
        s = src_ref[i, j]
        acc[s] += adj_ref[0, j].astype(F32)

    own = []
    for s in range(tiles):
        block = acc[s].astype(BF16)
        if s < own_tiles:
            own.append(block)
            cot_ref[s * rows : (s + 1) * rows, :] = block.T
        else:
            b = s - own_tiles
            cb_ref[:, b * rows : (b + 1) * rows] = block
            cbt_ref[b * rows : (b + 1) * rows, :] = block.T
    feats = feats_ref[...]
    own_ref[...] = dot(jnp.concatenate(own, axis=1), feats)
    mine = feats_ref[pl.ds(pl.multiple_of(i * rows, rows), rows), :]
    self_ref[...] = dot(mine, ws_ref[...])


def combine(tile_source_rows, tile_cnt, adj_tiles, feats, w_self, w_neigh, all_tiles):
    dst_tiles, slots, rows, _ = adj_tiles.shape
    nodes, width = feats.shape
    bnd = all_tiles * rows - nodes
    out_shape = [
        jax.ShapeDtypeStruct((nodes, bnd), BF16),
        jax.ShapeDtypeStruct((bnd, nodes), BF16),
        jax.ShapeDtypeStruct((nodes, nodes), BF16),
        jax.ShapeDtypeStruct((nodes, width), F32),
        jax.ShapeDtypeStruct((nodes, width), F32),
        jax.ShapeDtypeStruct((width, width), BF16),
        jax.ShapeDtypeStruct((width, width), BF16),
    ]
    return pl.pallas_call(
        combine_kernel,
        grid=(dst_tiles,),
        out_shape=out_shape,
        in_specs=[
            scalars(),
            scalars(),
            pl.BlockSpec((1, slots, rows, rows), lambda i: (i, 0, 0, 0)),
            whole((nodes, width)),
            whole((width, width)),
            whole((width, width)),
        ],
        out_specs=[
            pl.BlockSpec((rows, bnd), lambda i: (i, 0)),
            pl.BlockSpec((bnd, rows), lambda i: (0, i)),
            pl.BlockSpec((nodes, rows), lambda i: (0, i)),
            pl.BlockSpec((rows, width), lambda i: (i, 0)),
            pl.BlockSpec((rows, width), lambda i: (i, 0)),
            whole((width, width)),
            whole((width, width)),
        ],
        scratch_shapes=[pltpu.VMEM((all_tiles, rows, rows), F32)],
        compiler_params=PARAMS,
        cost_estimate=cost(nodes * width * (nodes + width), 20 * MIB),
        name="combine_tiles",
    )(tile_source_rows, tile_cnt, adj_tiles, feats, w_self, w_neigh)


class Stream:
    def __init__(self, copies, ahead):
        self.copies, self.ahead, self.started = copies, ahead, 0
        self.start(ahead)

    def start(self, count):
        while self.started < min(count, len(self.copies)):
            self.copies[self.started].start()
            self.started += 1

    def wait(self, *copies):
        for copy in copies:
            at = [c is copy for c in self.copies].index(True)
            self.start(at + 1 + self.ahead)
            copy.wait()


def layer_kernel(
    core_ref, cb_ref, in_ref, self_ref, own_ref, gout_ref, wn_ref, feats_ref,
    act_ref, gpre_ref, keep_ref, pass_ref,
    cb, rows_in, self_pre, own, gout, wn, feats, left, act, gpre, keep, give,
    cb_sems, in_sems, sems, out_sems,
):
    bnd, width = rows_in.shape
    cuts = [0, bnd // 8, bnd // 4, bnd // 2, 3 * bnd // 4, bnd]
    cuts = list(zip(cuts[:-1], cuts[1:]))
    spans = [pl.ds(a, b - a) for a, b in cuts]
    copy = pltpu.make_async_copy
    get_cb = [copy(cb_ref.at[:, d], cb.at[:, d], cb_sems.at[k]) for k, d in enumerate(spans)]
    get_in = [copy(in_ref.at[d], rows_in.at[d], in_sems.at[k]) for k, d in enumerate(spans)]
    rest = [
        (own_ref, own), (wn_ref, wn), (self_ref, self_pre), (gout_ref, gout),
        (feats_ref, feats),
    ]
    rest = [copy(src, dst, sems.at[n]) for n, (src, dst) in enumerate(rest)]
    loads = Stream([c for pair in zip(get_cb, get_in) for c in pair] + rest, 6)
    outs = []

    def put(src, dst):
        outs.append(copy(src, dst, out_sems.at[len(outs)]))
        outs[-1].start()

    total = None
    for k, (a, b) in enumerate(cuts):
        loads.wait(get_cb[k], get_in[k])
        term = dot(cb[:, a:b], rows_in[a:b, :])
        total = term if total is None else total + term
    loads.wait(rest[0])
    agg = (total + own[...]).astype(BF16)
    loads.wait(rest[1], rest[2])
    pre = self_pre[...] + dot(agg, wn[...])
    left[width:, :] = agg.T
    square = pre * pre
    t = jnp.tanh(GELU_SLOPE * pre * (1.0 + GELU_CUBIC * square))
    half = 0.5 * (1.0 + t)
    act[...] = (pre * half).astype(BF16)
    slope = half + 0.5 * pre * (1.0 - t * t) * (
        GELU_SLOPE * (1.0 + (3.0 * GELU_CUBIC) * square)
    )
    loads.wait(rest[3])
    gpre[...] = (gout[...].astype(F32) * slope).astype(BF16)
    put(act, act_ref)
    put(gpre, gpre_ref.at[0])
    loads.wait(rest[4])
    left[:width, :] = feats[...].T
    first = core_ref[0] == 0
    groups, halves, rows, lanes = keep.shape
    g = dot(left[...], gpre[...]).reshape(groups, rows, width)
    for h in range(halves):
        even = g[:, :, 2 * h * lanes : (2 * h + 1) * lanes]
        odd = g[:, :, (2 * h + 1) * lanes : (2 * h + 2) * lanes]
        keep[:, h] = jnp.where(first, even, odd)
        give[:, h] = jnp.where(first, odd, even).astype(BF16)
    put(give, pass_ref)
    put(keep, keep_ref)
    for c in outs:
        c.wait()


PLANES = 16


def layer(core, cb, incoming, self_pre, own_agg, grad_out, w_neigh, feats, chips):
    nodes, bnd = cb.shape
    width = incoming.shape[1]
    chunks = 5
    shares = (chips, width // (2 * LANES), 2 * width // chips, LANES)
    vmem = pltpu.VMEM
    sems = pltpu.SemaphoreType.DMA
    return pl.pallas_call(
        layer_kernel,
        out_shape=[
            jax.ShapeDtypeStruct((nodes, width), BF16),
            jax.ShapeDtypeStruct((PLANES, nodes, width), BF16),
            jax.ShapeDtypeStruct(shares, F32),
            jax.ShapeDtypeStruct(shares, BF16),
        ],
        in_specs=[scalars()] + [anywhere()] * 7,
        out_specs=[anywhere()] * 4,
        scratch_shapes=[
            vmem((nodes, bnd), BF16),
            vmem((bnd, width), BF16),
            vmem((nodes, width), F32),
            vmem((nodes, width), F32),
            vmem((nodes, width), BF16),
            vmem((width, width), BF16),
            vmem((nodes, width), BF16),
            vmem((2 * width, nodes), BF16),
            vmem((nodes, width), BF16),
            vmem((nodes, width), BF16),
            vmem(shares, F32),
            vmem(shares, BF16),
            sems((chunks,)),
            sems((chunks,)),
            sems((5,)),
            sems((4,)),
        ],
        compiler_params=LAYER_PARAMS,
        cost_estimate=cost(nodes * width * (bnd + 3 * width), 18 * MIB),
        name="layer",
    )(core, cb, incoming, self_pre, own_agg, grad_out, w_neigh, feats)


def boundary_kernel(
    cbt_ref, gpre_ref, wnt_ref, out_ref, gagg_ref,
    cbt, gpre, wnt, gagg, rows, cbt_sems, sems, out_sems,
):
    chunks = cbt_sems.shape[0]
    peers, slots, width = rows.shape
    nodes = gpre.shape[0]
    per, depth = peers // chunks, cbt.shape[0] // chunks
    copy = pltpu.make_async_copy
    get_w = copy(wnt_ref, wnt, sems.at[0])
    get_gpre = copy(gpre_ref.at[0], gpre, sems.at[1])
    get_cbt = [
        copy(cbt_ref.at[pl.ds(c * depth, depth)], cbt.at[pl.ds(c * depth, depth)], cbt_sems.at[c])
        for c in range(chunks)
    ]
    loads = Stream([get_w, get_gpre] + get_cbt, 3)
    outs = []

    def put(src, dst):
        outs.append(copy(src, dst, out_sems.at[len(outs)]))
        outs[-1].start()

    loads.wait(get_w, get_gpre)
    gagg[...] = dot(gpre[...], wnt[...]).astype(BF16)
    put(gagg, gagg_ref)
    for c in range(chunks):
        loads.wait(get_cbt[c])
        got = dot(cbt[c * depth : (c + 1) * depth, :], gagg[...]).astype(BF16)
        at = pl.ds(c * per, per)
        rows[at] = got.reshape(per, slots, width)
        put(rows.at[at], out_ref.at[at, :, pl.ds(0, width)])
    for c in outs:
        c.wait()


def boundary(cbt, grad_pre, w_neigh_t, peers, slots):
    bnd, nodes = cbt.shape
    width = grad_pre.shape[2]
    chunks = 4
    vmem = pltpu.VMEM
    return pl.pallas_call(
        boundary_kernel,
        out_shape=[
            jax.ShapeDtypeStruct((peers, slots, width + LANES), BF16),
            jax.ShapeDtypeStruct((nodes, width), BF16),
        ],
        in_specs=[anywhere()] * 3,
        out_specs=[anywhere()] * 2,
        scratch_shapes=[
            vmem((bnd, nodes), BF16),
            vmem((nodes, width), BF16),
            vmem((width, width), BF16),
            vmem((nodes, width), BF16),
            vmem((peers, slots, width), BF16),
            pltpu.SemaphoreType.DMA((chunks,)),
            pltpu.SemaphoreType.DMA((2,)),
            pltpu.SemaphoreType.DMA((chunks + 1,)),
        ],
        compiler_params=BACK_PARAMS,
        cost_estimate=cost((bnd + width) * nodes * width, 9 * MIB),
        name="boundary_grads",
    )(cbt, grad_pre, w_neigh_t)


def feats_grad_kernel(cot_ref, gagg_ref, gpre_ref, wst_ref, stale_ref, out_ref):
    total = dot(gpre_ref[0], wst_ref[...]) + dot(cot_ref[...], gagg_ref[...])
    out_ref[...] = (total + stale_ref[...].astype(F32)).astype(BF16)


def feats_grad(cot, grad_agg, grad_pre, w_self_t, stale_bgrad):
    nodes, width = grad_agg.shape
    block = 512
    by_block = lambda w: pl.BlockSpec((block, w), lambda i: (i, 0))
    return pl.pallas_call(
        feats_grad_kernel,
        grid=(nodes // block,),
        out_shape=jax.ShapeDtypeStruct((nodes, width), BF16),
        in_specs=[
            by_block(nodes),
            whole((nodes, width)),
            pl.BlockSpec((1, block, width), lambda i: (0, i, 0)),
            whole((width, width)),
            by_block(width),
        ],
        out_specs=by_block(width),
        compiler_params=PARAMS,
        cost_estimate=cost(nodes * width * (nodes + width), 7 * MIB),
        name="feats_grad",
    )(cot, grad_agg, grad_pre, w_self_t, stale_bgrad)


def add_kernel(keep_ref, got_ref, out_ref):
    out_ref[...] = (keep_ref[...] + got_ref[...].astype(F32)).astype(BF16)


def add_pair(keep, got):
    return pl.pallas_call(
        add_kernel,
        out_shape=jax.ShapeDtypeStruct(keep.shape, BF16),
        in_specs=[in_vmem()] * 2,
        out_specs=in_vmem(),
        compiler_params=SMALL_PARAMS,
        cost_estimate=cost(keep.size, 2 * MIB),
        name="add_pair",
    )(keep, got)


def take_kernel(ret_ref, out_ref):
    out_ref[...] = ret_ref[:, :, ret_ref.shape[2] - LANES :]


def take_shares(returned):
    peers, slots, _ = returned.shape
    return pl.pallas_call(
        take_kernel,
        out_shape=jax.ShapeDtypeStruct((peers, slots, LANES), BF16),
        in_specs=[in_vmem()],
        out_specs=in_vmem(),
        compiler_params=SMALL_PARAMS,
        cost_estimate=cost(peers * slots * LANES, MIB),
        name="take_shares",
    )(returned)


def share_kernel(parts_ref, _, out_ref, buf, sem):
    total = parts_ref[0].astype(F32)
    for c in range(1, parts_ref.shape[0]):
        total += parts_ref[c].astype(F32)
    total = total.astype(BF16)
    for p in range(buf.shape[0]):
        buf[p] = total[p % 2]
    width = out_ref.shape[2] - LANES
    copy = pltpu.make_async_copy(buf, out_ref.at[:, :, pl.ds(width, LANES)], sem)
    copy.start()
    copy.wait()


def lay_shares(parts, rows):
    peers, slots, _ = rows.shape
    return pl.pallas_call(
        share_kernel,
        out_shape=jax.ShapeDtypeStruct(rows.shape, BF16),
        in_specs=[in_vmem(), anywhere()],
        out_specs=anywhere(),
        scratch_shapes=[pltpu.VMEM((peers, slots, LANES), BF16), pltpu.SemaphoreType.DMA],
        input_output_aliases={1: 0},
        compiler_params=LAY_PARAMS,
        cost_estimate=cost(parts.size, MIB),
        name="lay_shares",
    )(parts, rows)


def slots_by_lane(idx, lanes):
    slots, peers = idx.shape
    per = lanes // slots
    tall = jnp.concatenate([idx] * per, axis=0).T
    peer = lax.broadcasted_iota(jnp.int32, tall.shape, 0)
    lane = lax.broadcasted_iota(jnp.int32, tall.shape, 1)
    return jnp.where(peer % per == lane // slots, tall, 0).reshape(peers // per, per, lanes).sum(axis=1)


def scatter_kernel(idx_ref, cnt_ref, ret_ref, out_ref, *, chunks):
    peers, slots, _ = ret_ref.shape
    nodes, width = out_ref.shape
    per = peers // chunks
    idx = slots_by_lane(live_slots(idx_ref, cnt_ref), LANES)
    node_ids = lax.broadcasted_iota(jnp.int32, (nodes, LANES), 0)
    count = per * slots // LANES
    total = None
    for c in range(chunks):
        picks = [
            jnp.where(idx[n : n + 1, :] == node_ids, 1.0, 0.0).astype(BF16)
            for n in range(c * count, (c + 1) * count)
        ]
        rows = ret_ref[c * per : (c + 1) * per, :, :width].reshape(per * slots, width)
        term = dot(jnp.concatenate(picks, axis=1), rows)
        total = term if total is None else total + term
    out_ref[...] = total.astype(BF16)


def scatter(slot_rows, send_cnt, returned, nodes, chunks=4):
    width = returned.shape[2] - LANES
    return pl.pallas_call(
        functools.partial(scatter_kernel, chunks=chunks),
        out_shape=jax.ShapeDtypeStruct((nodes, width), BF16),
        in_specs=[in_vmem()] * 3,
        out_specs=in_vmem(),
        compiler_params=SMALL_PARAMS,
        cost_estimate=cost(returned.size * nodes, 4 * MIB),
        name="scatter_rows",
    )(slot_rows, send_cnt, returned)


def weights_kernel(core_ref, mine_ref, other_ref, ws_ref, wn_ref):
    first = core_ref[0] == 0
    chips, halves, rows, lanes = mine_ref.shape
    for part, out_ref in enumerate((ws_ref, wn_ref)):
        at = pl.ds(part * (chips // 2), chips // 2)
        for h in range(halves):
            mine = mine_ref[at, h].astype(F32).reshape(chips // 2 * rows, lanes)
            other = other_ref[at, h].astype(F32).reshape(chips // 2 * rows, lanes)
            out_ref[:, h * lanes : (h + 1) * lanes] = jnp.where(first, mine, other)
            out_ref[:, (2 + h) * lanes : (3 + h) * lanes] = jnp.where(first, other, mine)


def lay_weights(core, mine, other, width):
    return pl.pallas_call(
        weights_kernel,
        out_shape=[jax.ShapeDtypeStruct((width, width), F32)] * 2,
        in_specs=[scalars()] + [in_vmem()] * 2,
        out_specs=[in_vmem()] * 2,
        compiler_params=SMALL_PARAMS,
        cost_estimate=cost(width * width, 3 * MIB),
        name="lay_weights",
    )(core, mine, other)


def body(
    feats,
    stale_feats,
    grad_out,
    stale_bgrad,
    w_self,
    w_neigh,
    adj_tiles,
    tile_source_rows,
    tile_cnt,
    send_idx,
    send_cnt,
):
    peers, slots = send_idx.shape
    nodes, width = feats.shape
    tile_rows = adj_tiles.shape[2]
    all_tiles = (nodes + peers * slots) // tile_rows
    chips = peers // 2
    core = lax.rem(lax.axis_index("dom"), 2).astype(jnp.int32).reshape(1)
    pairs = [(d, d + 1 - 2 * (d % 2)) for d in range(peers)]
    same_core = [list(range(c, peers, 2)) for c in range(2)]

    def exchange(v, groups):
        return lax.all_to_all(
            v, "dom", split_axis=0, concat_axis=0, tiled=True, axis_index_groups=groups
        )

    slot_rows = send_idx.T
    outgoing = gather(slot_rows, send_cnt, stale_feats)
    incoming = exchange(outgoing, None).reshape(peers * slots, width)
    cb, cbt, cot, self_pre, own_agg, w_self_t, w_neigh_t = combine(
        tile_source_rows, tile_cnt, adj_tiles, feats, w_self, w_neigh, all_tiles
    )
    activated, grad_pre, keep, give = layer(
        core, cb, incoming, self_pre, own_agg, grad_out, w_neigh, feats, chips
    )
    got = lax.ppermute(give, "dom", pairs)
    parts = exchange(add_pair(keep, got), same_core)
    rows, grad_agg = boundary(cbt, grad_pre, w_neigh_t, peers, slots)
    returned = exchange(lay_shares(parts, rows), None)
    grad_feats = feats_grad(cot, grad_agg, grad_pre, w_self_t, stale_bgrad)
    returned, grad_feats = lax.optimization_barrier((returned, grad_feats))

    mine = take_shares(returned).reshape(keep.shape)
    other = lax.ppermute(mine, "dom", pairs)
    next_bgrad = scatter(slot_rows, send_cnt, returned, nodes)
    grad_w_self, grad_w_neigh = lay_weights(core, mine, other, width)
    return activated, grad_feats, next_bgrad, grad_w_self, grad_w_neigh


def solution(mesh):
    in_specs = (
        P("dom", None),
        P("dom", None),
        P("dom", None),
        P("dom", None),
        P(),
        P(),
        P("dom", None, None, None),
        P("dom", None),
        P("dom"),
        P("dom", None),
        P("dom", None),
    )
    out_specs = (P("dom", None), P("dom", None), P("dom", None), P(), P())
    return jax.shard_map(body, mesh=mesh, in_specs=in_specs, out_specs=out_specs, check_vma=False)
```

profile of v0, /device:TPU:1, one launch (start us, length us, event | category | flops | bytes accessed | tf_op | source)
XLA Modules:
  0.0 124.6 jit_solution(6486433352446145814)
XLA Ops:
  0.6 5.1 %gather_rows.1 = bf16[128,16,512]{2,1,0:T(8,128)(2,1)} custom-call(s32[16,128]{1,0:T(8,128)} %bitcast.6, s32[1,128]{1,0:T(1,128)} %cnt_ref.5, bf16[1024,512]{1,0:T(8,128)(2,1)} %rows_ref.1), custom_call_target="tpu_custom_call" | custom-call | flops 2147483648 | bytes 3145728 | tf_op jit(solution)/shard_map/gather_rows/pallas_call | solution.py:87
  5.8 12.0 %all-to-all-start = ((bf16[128,16,512]{2,1,0:T(8,128)(2,1)}), bf16[128,16,512]{2,1,0:T(8,128)(2,1)}, u32[]{:S(2)}, u32[]{:S(2)}) async-start(bf16[128,16,512]{2,1,0:T(8,128)(2,1)} %gather_rows.1), calls=%async_computation | async-start | bytes 4194304 | tf_op jit(solution)/shard_map/all_to_all | solution.py:544
  17.7 0.0 copy-start
  17.8 0.0 copy-start.1
  17.8 0.0 copy-start.2
  17.8 11.4 %combine_tiles.1 = (bf16[1024,2048]{1,0:T(8,128)(2,1)}, bf16[2048,1024]{1,0:T(8,128)(2,1)}, bf16[1024,1024]{1,0:T(8,128)(2,1)}, f32[1024,512]{1,0:T(8,128)}, f32...) custom-call(s32[8,16]{1,0:T(8,128)} %src_ref.1, s32[8]{0:T(128)} %cnt_ref.3, ...), custom_call_target="tpu_custom_call" | custom-call | flops 1610612736 | bytes 20971520 | tf_op jit(solution)/shard_map/combine_tiles/pallas_call | solution.py:153
  29.2 18.6 %all-to-all-done = bf16[128,16,512]{2,1,0:T(8,128)(2,1)} async-done(((bf16[128,16,512]{2,1,0:T(8,128)(2,1)}), bf16[128,16,512]{2,1,0:T(8,128)(2,1)}, u32[]{:S(2)}, u32[]{:S(2)}) %all-to-all-start) | async-done | bytes 2097184 | tf_op jit(solution)/shard_map/all_to_all | solution.py:544
  47.8 0.0 copy-done
  47.8 0.0 copy-done.1
  47.8 0.0 copy-done.2
  47.8 7.8 %layer.1 = (bf16[1024,512]{1,0:T(8,128)(2,1)}, bf16[16,1024,512]{2,1,0:T(8,128)(2,1)}, f32[64,2,16,128]{3,2,1,0:T(8,128)S(1)}, bf16[64,2,16,128]{3,2,1,0:T(8,128)(2,1)S(1)}) custom-call(s32[1]{0:T(128)} %bitcast.core_ref, bf16[1024,2048]{1,0:T(8,128)(2,1)} %get-tuple-element.22.cb_ref, bf16[2048,512]{1,0:T(8,128)(2,1)} %bitcast.2.in_ref, ...), custom_call_target="tpu_custom_call" | custom-call | flops 3758096384 | bytes 18874368 | tf_op jit(solution)/shard_map/layer/pallas_call | solution.py:270
  55.6 1.2 collective-permute-start
  56.8 1.5 %collective-permute-done.got_ref = bf16[64,2,16,128]{3,2,1,0:T(8,128)(2,1)S(1)} collective-permute-done((bf16[64,2,16,128]{3,2,1,0:T(8,128)(2,1)S(1)}, bf16[64,2,16,128]{3,2,1,0:T(8,128)(2,1)S(1)}, u32[]{:S(2)}, u32[]{:S(2)}) %collective-permute-start) | collective-permute-done | bytes 524320 | tf_op jit(solution)/shard_map/ppermute | solution.py:557
  58.4 0.9 add_pair.1
  59.2 4.6 %all-to-all-start.1 = ((bf16[64,2,16,128]{3,2,1,0:T(8,128)(2,1)}), bf16[64,2,16,128]{3,2,1,0:T(8,128)(2,1)S(1)}, u32[]{:S(2)}, u32[]{:S(2)}) async-start(bf16[64,2,16,128]{3,2,1,0:T(8,128)(2,1)} %add_pair.1), calls=%async_computation.1 | async-start | bytes 1048576 | tf_op jit(solution)/shard_map/all_to_all | solution.py:544
  63.9 6.2 %boundary_grads.1 = (bf16[128,16,640]{2,1,0:T(8,128)(2,1)}, bf16[1024,512]{1,0:T(8,128)(2,1)}) custom-call(bf16[2048,1024]{1,0:T(8,128)(2,1)} %get-tuple-element.28.cbt_ref, bf16[16,1024,512]{2,1,0:T(8,128)(2,1)} %get-tuple-element.29.gpre_ref, bf16[512,512]{1,0:T(8,128)(2,1)} %get-tuple-element.30.wnt_ref), custom_call_target="tpu_custom_call" | custom-call | flops 2684354560 | bytes 9437184 | tf_op jit(solution)/shard_map/boundary_grads/pallas_call | solution.py:344
  70.1 6.0 %all-to-all-done.1.parts_ref = bf16[64,2,16,128]{3,2,1,0:T(8,128)(2,1)S(1)} async-done(((bf16[64,2,16,128]{3,2,1,0:T(8,128)(2,1)}), bf16[64,2,16,128]{3,2,1,0:T(8,128)(2,1)S(1)}, u32[]{:S(2)}, u32[]{:S(2)}) %all-to-all-start.1) | async-done | bytes 524320 | tf_op jit(solution)/shard_map/all_to_all | solution.py:544
  76.0 0.9 lay_shares.1
  77.0 5.4 %all-to-all-start.2 = ((bf16[128,16,640]{2,1,0:T(8,128)(2,1)}), bf16[128,16,640]{2,1,0:T(8,128)(2,1)S(1)}, u32[]{:S(2)}, u32[]{:S(2)}) async-start(bf16[128,16,640]{2,1,0:T(8,128)(2,1)} %lay_shares.1), calls=%async_computation.2 | async-start | bytes 5242880 | tf_op jit(solution)/shard_map/all_to_all | solution.py:544
  82.4 5.0 %feats_grad.1 = bf16[1024,512]{1,0:T(8,128)(2,1)} custom-call(bf16[1024,1024]{1,0:T(8,128)(2,1)} %get-tuple-element.32.cot_ref, bf16[1024,512]{1,0:T(8,128)(2,1)} %get-tuple-element.33.gagg_ref, bf16[16,1024,512]{2,1,0:T(8,128)(2,1)} %get-tuple-element.29.gpre_ref, bf16[512,512]{1,0:T(8,128)(2,1)} %get-tuple-element.34.wst_ref, bf16[1024,512]{1,0:T(8,128)(2,1)} %stale_ref.1), custom_call_target="tpu_custom_call" | custom-call | flops 1610612736 | bytes 7340032 | tf_op jit(solution)/shard_map/feats_grad/pallas_call | solution.py:377
  87.3 0.0 copy-start.3
  87.3 0.0 copy-start.4
  87.3 31.3 %all-to-all-done.2.ret_ref = bf16[128,16,640]{2,1,0:T(8,128)(2,1)S(1)} async-done(((bf16[128,16,640]{2,1,0:T(8,128)(2,1)}), bf16[128,16,640]{2,1,0:T(8,128)(2,1)S(1)}, u32[]{:S(2)}, u32[]{:S(2)}) %all-to-all-start.2) | async-done | bytes 2621472 | tf_op jit(solution)/shard_map/all_to_all | solution.py:544
  118.6 0.1 take_shares.1
  118.7 1.1 collective-permute-start.1
  119.8 0.0 copy-done.3
  119.8 0.0 copy-done.4
  119.8 3.3 %scatter_rows.1 = bf16[1024,512]{1,0:T(8,128)(2,1)} custom-call(s32[16,128]{1,0:T(8,128)S(1)} %bitcast.7, s32[1,128]{1,0:T(1,128)S(1)} %copy-done.4, bf16[128,16,640]{2,1,0:T(8,128)(2,1)S(1)} %all-to-all-done.2.ret_ref), custom_call_target="tpu_custom_call" | custom-call | flops 2684354560 | bytes 4194304 | tf_op jit(solution)/shard_map/scatter_rows/pallas_call | solution.py:486
  123.2 0.0 collective-permute-done.1.other_ref
  123.2 1.5 %lay_weights.1 = (f32[512,512]{1,0:T(8,128)}, f32[512,512]{1,0:T(8,128)}) custom-call(s32[1]{0:T(128)} %bitcast.core_ref, bf16[64,2,16,128]{3,2,1,0:T(8,128)(2,1)S(1)} %bitcast.5, bf16[64,2,16,128]{3,2,1,0:T(8,128)(2,1)S(1)} %collective-permute-done.1.other_ref), custom_call_target="tpu_custom_call" | custom-call | flops 524288 | bytes 3145728 | tf_op jit(solution)/shard_map/lay_weights/pallas_call | solution.py:510
Async XLA Ops:
  5.8 42.0 %all-to-all-start = ((bf16[128,16,512]{2,1,0:T(8,128)(2,1)}), bf16[128,16,512]{2,1,0:T(8,128)(2,1)}, u32[]{:S(2)}, u32[]{:S(2)}) async-start(bf16[128,16,512]{2,1,0:T(8,128)(2,1)} %gather_rows.1), calls=%async_computation | async-start | bytes 4194304 | tf_op jit(solution)/shard_map/all_to_all | solution.py:544
  17.7 30.0 %copy-start = (bf16[1024,512]{1,0:T(8,128)(2,1)S(1)}, bf16[1024,512]{1,0:T(8,128)(2,1)}, u32[]{:S(2)}) copy-start(bf16[1024,512]{1,0:T(8,128)(2,1)} %feats_ref.3) | copy-start | bytes 3145732
  17.8 30.0 %copy-start.1 = (bf16[512,512]{1,0:T(8,128)(2,1)S(1)}, bf16[512,512]{1,0:T(8,128)(2,1)}, u32[]{:S(2)}) copy-start(bf16[512,512]{1,0:T(8,128)(2,1)} %wn_ref.3) | copy-start | bytes 1572868
  17.8 30.0 %copy-start.2 = (bf16[1024,512]{1,0:T(8,128)(2,1)S(1)}, bf16[1024,512]{1,0:T(8,128)(2,1)}, u32[]{:S(2)}) copy-start(bf16[1024,512]{1,0:T(8,128)(2,1)} %gout_ref.1) | copy-start | bytes 3145732
  55.6 2.7 %collective-permute-start = (bf16[64,2,16,128]{3,2,1,0:T(8,128)(2,1)S(1)}, bf16[64,2,16,128]{3,2,1,0:T(8,128)(2,1)S(1)}, u32[]{:S(2)}, u32[]{:S(2)}) collective-permute-start(bf16[64,2,16,128]{3,2,1,0:T(8,128)(2,1)S(1)} %get-tuple-element.27), channel_id=1, source_target_pairs={{0,1},{1,0},{2,3},{3,2},{4,5},{5,4},{6,7},{7,6},{8,9},{9,8},{10,11... | collective-permute-start | bytes 1572872 | tf_op jit(solution)/shard_map/ppermute | solution.py:557
  59.2 16.8 %all-to-all-start.1 = ((bf16[64,2,16,128]{3,2,1,0:T(8,128)(2,1)}), bf16[64,2,16,128]{3,2,1,0:T(8,128)(2,1)S(1)}, u32[]{:S(2)}, u32[]{:S(2)}) async-start(bf16[64,2,16,128]{3,2,1,0:T(8,128)(2,1)} %add_pair.1), calls=%async_computation.1 | async-start | bytes 1048576 | tf_op jit(solution)/shard_map/all_to_all | solution.py:544
  77.0 41.6 %all-to-all-start.2 = ((bf16[128,16,640]{2,1,0:T(8,128)(2,1)}), bf16[128,16,640]{2,1,0:T(8,128)(2,1)S(1)}, u32[]{:S(2)}, u32[]{:S(2)}) async-start(bf16[128,16,640]{2,1,0:T(8,128)(2,1)} %lay_shares.1), calls=%async_computation.2 | async-start | bytes 5242880 | tf_op jit(solution)/shard_map/all_to_all | solution.py:544
  87.3 32.5 %copy-start.3 = (s32[128,16]{0,1:T(8,128)S(1)}, s32[128,16]{0,1:T(8,128)}, u32[]{:S(2)}) copy-start(s32[128,16]{0,1:T(8,128)} %param.20) | copy-start | bytes 24580
  87.3 32.5 %copy-start.4 = (s32[1,128]{1,0:T(1,128)S(1)}, s32[1,128]{1,0:T(1,128)}, u32[]{:S(2)}) copy-start(s32[1,128]{1,0:T(1,128)} %cnt_ref.5) | copy-start | bytes 1540
  118.7 4.5 %collective-permute-start.1 = (bf16[64,2,16,128]{3,2,1,0:T(8,128)(2,1)S(1)}, bf16[64,2,16,128]{3,2,1,0:T(8,128)(2,1)S(1)}, u32[]{:S(2)}, u32[]{:S(2)}) collective-permute-start(bf16[64,2,16,128]{3,2,1,0:T(8,128)(2,1)S(1)} %bitcast.4), channel_id=1, source_target_pairs={{0,1},{1,0},{2,3},{3,2},{4,5},{5,4},{6,7},{7,6},{8,9},{9,8},{10,11... | collective-permute-start | bytes 1572872 | tf_op jit(solution)/shard_map/ppermute | solution.py:565
where the time goes:
time: 125 us
  waiting for transfers between devices  57.3 us (46%)
  Pallas kernels  42.3 us (34%)
  starting transfers between devices  24.3 us (19%)
    all_to_all x3, waiting for transfers between devices, exchange(): lax.all_to_all(v, 'dom', split_axis=0, concat_axis=0, tiled=True, axis_in...  55.8 us
    all_to_all x3, starting transfers between devices, exchange(): lax.all_to_all(v, 'dom', split_axis=0, concat_axis=0, tiled=True, axis_in...  22 us
    pallas_call x1, Pallas kernels, combine(): pl.pallas_call(combine_kernel, grid=(dst_tiles,), out_shape=out_shape, in...  11.4 us
    pallas_call x1, Pallas kernels, layer(): pl.pallas_call(layer_kernel, out_shape=[jax.ShapeDtypeStruct((nodes, widt...  7.82 us
    pallas_call x1, Pallas kernels, boundary(): pl.pallas_call(boundary_kernel, out_shape=[jax.ShapeDtypeStruct((peers, s...  6.2 us
    pallas_call x1, Pallas kernels, gather(): pl.pallas_call(functools.partial(gather_kernel, groups=groups), out_shape...  5.13 us
    pallas_call x1, Pallas kernels, feats_grad(): pl.pallas_call(feats_grad_kernel, grid=(nodes // block,), out_shape=jax.S...  4.95 us
    pallas_call x1, Pallas kernels, scatter(): pl.pallas_call(functools.partial(scatter_kernel, chunks=chunks), out_shap...  3.35 us
  transfers between devices with their start and end apart: 5, of which 4 were waited for; matrix products, arithmetic and copies ran while one was open for 0% of the time, Pallas kernels for 21%

commit v1 on v0

--- a/solution.py
+++ b/solution.py
@@ -44,6 +44,10 @@
 
 def cost(macs, moved):
     return pl.CostEstimate(flops=2 * macs, bytes_accessed=moved, transcendentals=0)
+
+
+def first_core():
+    return lax.rem(lax.axis_index("dom"), 2) == 0
 
 
 def live_slots(idx_ref, cnt_ref):
@@ -60,18 +64,27 @@
     return jnp.concatenate(picks, axis=0)
 
 
-def gather_kernel(idx_ref, cnt_ref, rows_ref, out_ref, rows, buf, sem, sems, *, groups):
-    slots, peers = idx_ref.shape
+def gather_kernel(
+    idx_ref, cnt_ref, rows_ref, out_ref, slot_idx, slot_cnt, rows, buf, load_sems, sems
+):
+    groups = sems.shape[0]
+    slots, peers = slot_idx.shape
     nodes, width = rows.shape
-    load = pltpu.make_async_copy(rows_ref, rows, sem)
-    load.start()
-    idx = live_slots(idx_ref, cnt_ref)
+    pairs = ((idx_ref, slot_idx), (cnt_ref, slot_cnt), (rows_ref, rows))
+    loads = [
+        pltpu.make_async_copy(src, dst, load_sems.at[n]) for n, (src, dst) in enumerate(pairs)
+    ]
+    for load in loads:
+        load.start()
+    loads[0].wait()
+    loads[1].wait()
+    idx = live_slots(slot_idx, slot_cnt)
     per = peers // groups
     copies = []
     for g in range(groups):
         picks = one_hot(idx, nodes, g * per, per)
         if g == 0:
-            load.wait()
+            loads[2].wait()
         span = pl.ds(g * per, per)
         buf[span] = dot(picks, rows[...]).astype(BF16).reshape(per, slots, width)
         copy = pltpu.make_async_copy(buf.at[span], out_ref.at[span], sems.at[g])
@@ -85,14 +98,16 @@
     slots, peers = slot_rows.shape
     nodes, width = stale_feats.shape
     return pl.pallas_call(
-        functools.partial(gather_kernel, groups=groups),
+        gather_kernel,
         out_shape=jax.ShapeDtypeStruct((peers, slots, width), BF16),
-        in_specs=[in_vmem()] * 2 + [anywhere()],
+        in_specs=[anywhere()] * 3,
         out_specs=anywhere(),
         scratch_shapes=[
+            pltpu.VMEM((slots, peers), jnp.int32),
+            pltpu.VMEM((1, peers), jnp.int32),
             pltpu.VMEM((nodes, width), BF16),
             pltpu.VMEM((peers, slots, width), BF16),
-            pltpu.SemaphoreType.DMA,
+            pltpu.SemaphoreType.DMA((3,)),
             pltpu.SemaphoreType.DMA((groups,)),
         ],
         compiler_params=PARAMS,
@@ -196,7 +211,7 @@
 
 
 def layer_kernel(
-    core_ref, cb_ref, in_ref, self_ref, own_ref, gout_ref, wn_ref, feats_ref,
+    cb_ref, in_ref, self_ref, own_ref, gout_ref, wn_ref, feats_ref,
     act_ref, gpre_ref, keep_ref, pass_ref,
     cb, rows_in, self_pre, own, gout, wn, feats, left, act, gpre, keep, give,
     cb_sems, in_sems, sems, out_sems,
@@ -243,7 +258,7 @@
     put(gpre, gpre_ref.at[0])
     loads.wait(rest[4])
     left[:width, :] = feats[...].T
-    first = core_ref[0] == 0
+    first = first_core()
     groups, halves, rows, lanes = keep.shape
     g = dot(left[...], gpre[...]).reshape(groups, rows, width)
     for h in range(halves):
@@ -260,7 +275,7 @@
 PLANES = 16
 
 
-def layer(core, cb, incoming, self_pre, own_agg, grad_out, w_neigh, feats, chips):
+def layer(cb, incoming, self_pre, own_agg, grad_out, w_neigh, feats, chips):
     nodes, bnd = cb.shape
     width = incoming.shape[1]
     chunks = 5
@@ -275,7 +290,7 @@
             jax.ShapeDtypeStruct(shares, F32),
             jax.ShapeDtypeStruct(shares, BF16),
         ],
-        in_specs=[scalars()] + [anywhere()] * 7,
+        in_specs=[anywhere()] * 7,
         out_specs=[anywhere()] * 4,
         scratch_shapes=[
             vmem((nodes, bnd), BF16),
@@ -298,7 +313,7 @@
         compiler_params=LAYER_PARAMS,
         cost_estimate=cost(nodes * width * (bnd + 3 * width), 18 * MIB),
         name="layer",
-    )(core, cb, incoming, self_pre, own_agg, grad_out, w_neigh, feats)
+    )(cb, incoming, self_pre, own_agg, grad_out, w_neigh, feats)
 
 
 def boundary_kernel(
@@ -494,8 +509,8 @@
     )(slot_rows, send_cnt, returned)
 
 
-def weights_kernel(core_ref, mine_ref, other_ref, ws_ref, wn_ref):
-    first = core_ref[0] == 0
+def weights_kernel(mine_ref, other_ref, ws_ref, wn_ref):
+    first = first_core()
     chips, halves, rows, lanes = mine_ref.shape
     for part, out_ref in enumerate((ws_ref, wn_ref)):
         at = pl.ds(part * (chips // 2), chips // 2)
@@ -506,16 +521,16 @@
             out_ref[:, (2 + h) * lanes : (3 + h) * lanes] = jnp.where(first, other, mine)
 
 
-def lay_weights(core, mine, other, width):
+def lay_weights(mine, other, width):
     return pl.pallas_call(
         weights_kernel,
         out_shape=[jax.ShapeDtypeStruct((width, width), F32)] * 2,
-        in_specs=[scalars()] + [in_vmem()] * 2,
+        in_specs=[in_vmem()] * 2,
         out_specs=[in_vmem()] * 2,
         compiler_params=SMALL_PARAMS,
         cost_estimate=cost(width * width, 3 * MIB),
         name="lay_weights",
-    )(core, mine, other)
+    )(mine, other)
 
 
 def body(
@@ -536,7 +551,6 @@
     tile_rows = adj_tiles.shape[2]
     all_tiles = (nodes + peers * slots) // tile_rows
     chips = peers // 2
-    core = lax.rem(lax.axis_index("dom"), 2).astype(jnp.int32).reshape(1)
     pairs = [(d, d + 1 - 2 * (d % 2)) for d in range(peers)]
     same_core = [list(range(c, peers, 2)) for c in range(2)]
 
@@ -552,7 +566,7 @@
         tile_source_rows, tile_cnt, adj_tiles, feats, w_self, w_neigh, all_tiles
     )
     activated, grad_pre, keep, give = layer(
-        core, cb, incoming, self_pre, own_agg, grad_out, w_neigh, feats, chips
+        cb, incoming, self_pre, own_agg, grad_out, w_neigh, feats, chips
     )
     got = lax.ppermute(give, "dom", pairs)
     parts = exchange(add_pair(keep, got), same_core)
@@ -564,7 +578,7 @@
     mine = take_shares(returned).reshape(keep.shape)
     other = lax.ppermute(mine, "dom", pairs)
     next_bgrad = scatter(slot_rows, send_cnt, returned, nodes)
-    grad_w_self, grad_w_neigh = lay_weights(core, mine, other, width)
+    grad_w_self, grad_w_neigh = lay_weights(mine, other, width)
     return activated, grad_feats, next_bgrad, grad_w_self, grad_w_neigh
 
 

time: 125 us -> 125 us (level)
  no operation moved by 1% of the time
where the time goes in v1:
time: 125 us; the launch traced here: 124 us
  waiting for transfers between devices  57.4 us (46%)
  Pallas kernels  41.6 us (33%)
  starting transfers between devices  24.3 us (19%)
    all_to_all x3, waiting for transfers between devices, exchange(): lax.all_to_all(v, 'dom', split_axis=0, concat_axis=0, tiled=True, axis_in...  55.8 us
    all_to_all x3, starting transfers between devices, exchange(): lax.all_to_all(v, 'dom', split_axis=0, concat_axis=0, tiled=True, axis_in...  22 us
    pallas_call x1, Pallas kernels, combine(): pl.pallas_call(combine_kernel, grid=(dst_tiles,), out_shape=out_shape, in...  11.4 us
    pallas_call x1, Pallas kernels, layer(): pl.pallas_call(layer_kernel, out_shape=[jax.ShapeDtypeStruct((nodes, widt...  7.81 us
    pallas_call x1, Pallas kernels, boundary(): pl.pallas_call(boundary_kernel, out_shape=[jax.ShapeDtypeStruct((peers, s...  6.2 us
    pallas_call x1, Pallas kernels, feats_grad(): pl.pallas_call(feats_grad_kernel, grid=(nodes // block,), out_shape=jax.S...  4.95 us
    pallas_call x1, Pallas kernels, gather(): pl.pallas_call(gather_kernel, out_shape=jax.ShapeDtypeStruct((peers, slot...  4.48 us
    pallas_call x1, Pallas kernels, scatter(): pl.pallas_call(functools.partial(scatter_kernel, chunks=chunks), out_shap...  3.35 us
  transfers between devices with their start and end apart: 5, of which 4 were waited for; matrix products, arithmetic and copies ran while one was open for 0% of the time, Pallas kernels for 21%

profile of v1, /device:TPU:1, one launch (start us, length us, event | category | flops | bytes accessed | tf_op | source)
XLA Modules:
  0.0 124.0 jit_solution(441690463808304709)
XLA Ops:
  0.6 4.5 %gather_rows.1 = bf16[128,16,512]{2,1,0:T(8,128)(2,1)} custom-call(s32[16,128]{1,0:T(8,128)} %bitcast.5, s32[1,128]{1,0:T(1,128)} %cnt_ref.5, bf16[1024,512]{1,0:T(8,128)(2,1)} %rows_ref.1), custom_call_target="tpu_custom_call" | custom-call | flops 2147483648 | bytes 3145728 | tf_op jit(solution)/shard_map/gather_rows/pallas_call | solution.py:100
  5.1 12.0 %all-to-all-start = ((bf16[128,16,512]{2,1,0:T(8,128)(2,1)}), bf16[128,16,512]{2,1,0:T(8,128)(2,1)}, u32[]{:S(2)}, u32[]{:S(2)}) async-start(bf16[128,16,512]{2,1,0:T(8,128)(2,1)} %gather_rows.1), calls=%async_computation | async-start | bytes 4194304 | tf_op jit(solution)/shard_map/all_to_all | solution.py:558
  17.1 0.0 copy-start
  17.1 0.0 copy-start.1
  17.1 0.0 copy-start.2
  17.1 11.4 %combine_tiles.1 = (bf16[1024,2048]{1,0:T(8,128)(2,1)}, bf16[2048,1024]{1,0:T(8,128)(2,1)}, bf16[1024,1024]{1,0:T(8,128)(2,1)}, f32[1024,512]{1,0:T(8,128)}, f32...) custom-call(s32[8,16]{1,0:T(8,128)} %src_ref.1, s32[8]{0:T(128)} %cnt_ref.3, ...), custom_call_target="tpu_custom_call" | custom-call | flops 1610612736 | bytes 20971520 | tf_op jit(solution)/shard_map/combine_tiles/pallas_call | solution.py:168
  28.5 18.6 %all-to-all-done = bf16[128,16,512]{2,1,0:T(8,128)(2,1)} async-done(((bf16[128,16,512]{2,1,0:T(8,128)(2,1)}), bf16[128,16,512]{2,1,0:T(8,128)(2,1)}, u32[]{:S(2)}, u32[]{:S(2)}) %all-to-all-start) | async-done | bytes 2097184 | tf_op jit(solution)/shard_map/all_to_all | solution.py:558
  47.1 0.0 copy-done
  47.1 0.0 copy-done.1
  47.1 0.0 copy-done.2
  47.1 7.8 %layer.1 = (bf16[1024,512]{1,0:T(8,128)(2,1)}, bf16[16,1024,512]{2,1,0:T(8,128)(2,1)}, f32[64,2,16,128]{3,2,1,0:T(8,128)S(1)}, bf16[64,2,16,128]{3,2,1,0:T(8,128)(2,1)S(1)}) custom-call(bf16[1024,2048]{1,0:T(8,128)(2,1)} %get-tuple-element.22.cb_ref, bf16[2048,512]{1,0:T(8,128)(2,1)} %bitcast.1.in_ref, f32[1024,512]{1,0:T(8,128)} %get-tuple-element.23.self_ref, ...), custom_call_target="tpu_custom_call" | custom-call | flops 3758096384 | bytes 18874368 | tf_op jit(solution)/shard_map/layer/pallas_call | solution.py:285
  55.0 1.2 collective-permute-start
  56.2 1.5 %collective-permute-done.got_ref = bf16[64,2,16,128]{3,2,1,0:T(8,128)(2,1)S(1)} collective-permute-done((bf16[64,2,16,128]{3,2,1,0:T(8,128)(2,1)S(1)}, bf16[64,2,16,128]{3,2,1,0:T(8,128)(2,1)S(1)}, u32[]{:S(2)}, u32[]{:S(2)}) %collective-permute-start) | collective-permute-done | bytes 524320 | tf_op jit(solution)/shard_map/ppermute | solution.py:571
  57.7 0.9 add_pair.1
  58.6 4.6 %all-to-all-start.1 = ((bf16[64,2,16,128]{3,2,1,0:T(8,128)(2,1)}), bf16[64,2,16,128]{3,2,1,0:T(8,128)(2,1)S(1)}, u32[]{:S(2)}, u32[]{:S(2)}) async-start(bf16[64,2,16,128]{3,2,1,0:T(8,128)(2,1)} %add_pair.1), calls=%async_computation.1 | async-start | bytes 1048576 | tf_op jit(solution)/shard_map/all_to_all | solution.py:558
  63.2 6.2 %boundary_grads.1 = (bf16[128,16,640]{2,1,0:T(8,128)(2,1)}, bf16[1024,512]{1,0:T(8,128)(2,1)}) custom-call(bf16[2048,1024]{1,0:T(8,128)(2,1)} %get-tuple-element.28.cbt_ref, bf16[16,1024,512]{2,1,0:T(8,128)(2,1)} %get-tuple-element.29.gpre_ref, bf16[512,512]{1,0:T(8,128)(2,1)} %get-tuple-element.30.wnt_ref), custom_call_target="tpu_custom_call" | custom-call | flops 2684354560 | bytes 9437184 | tf_op jit(solution)/shard_map/boundary_grads/pallas_call | solution.py:359
  69.4 6.0 %all-to-all-done.1.parts_ref = bf16[64,2,16,128]{3,2,1,0:T(8,128)(2,1)S(1)} async-done(((bf16[64,2,16,128]{3,2,1,0:T(8,128)(2,1)}), bf16[64,2,16,128]{3,2,1,0:T(8,128)(2,1)S(1)}, u32[]{:S(2)}, u32[]{:S(2)}) %all-to-all-start.1) | async-done | bytes 524320 | tf_op jit(solution)/shard_map/all_to_all | solution.py:558
  75.4 0.9 lay_shares.1
  76.3 5.4 %all-to-all-start.2 = ((bf16[128,16,640]{2,1,0:T(8,128)(2,1)}), bf16[128,16,640]{2,1,0:T(8,128)(2,1)S(1)}, u32[]{:S(2)}, u32[]{:S(2)}) async-start(bf16[128,16,640]{2,1,0:T(8,128)(2,1)} %lay_shares.1), calls=%async_computation.2 | async-start | bytes 5242880 | tf_op jit(solution)/shard_map/all_to_all | solution.py:558
  81.7 5.0 %feats_grad.1 = bf16[1024,512]{1,0:T(8,128)(2,1)} custom-call(bf16[1024,1024]{1,0:T(8,128)(2,1)} %get-tuple-element.32.cot_ref, bf16[1024,512]{1,0:T(8,128)(2,1)} %get-tuple-element.33.gagg_ref, bf16[16,1024,512]{2,1,0:T(8,128)(2,1)} %get-tuple-element.29.gpre_ref, bf16[512,512]{1,0:T(8,128)(2,1)} %get-tuple-element.34.wst_ref, bf16[1024,512]{1,0:T(8,128)(2,1)} %stale_ref.1), custom_call_target="tpu_custom_call" | custom-call | flops 1610612736 | bytes 7340032 | tf_op jit(solution)/shard_map/feats_grad/pallas_call | solution.py:392
  86.7 0.0 copy-start.3
  86.7 0.0 copy-start.4
  86.7 31.2 %all-to-all-done.2.ret_ref = bf16[128,16,640]{2,1,0:T(8,128)(2,1)S(1)} async-done(((bf16[128,16,640]{2,1,0:T(8,128)(2,1)}), bf16[128,16,640]{2,1,0:T(8,128)(2,1)S(1)}, u32[]{:S(2)}, u32[]{:S(2)}) %all-to-all-start.2) | async-done | bytes 2621472 | tf_op jit(solution)/shard_map/all_to_all | solution.py:558
  117.9 0.1 take_shares.1
  118.0 1.1 collective-permute-start.1
  119.1 0.0 copy-done.3
  119.1 0.0 copy-done.4
  119.2 3.3 %scatter_rows.1 = bf16[1024,512]{1,0:T(8,128)(2,1)} custom-call(s32[16,128]{1,0:T(8,128)S(1)} %bitcast.6, s32[1,128]{1,0:T(1,128)S(1)} %copy-done.4, bf16[128,16,640]{2,1,0:T(8,128)(2,1)S(1)} %all-to-all-done.2.ret_ref), custom_call_target="tpu_custom_call" | custom-call | flops 2684354560 | bytes 4194304 | tf_op jit(solution)/shard_map/scatter_rows/pallas_call | solution.py:501
  122.5 0.0 collective-permute-done.1.other_ref
  122.5 1.5 %lay_weights.1 = (f32[512,512]{1,0:T(8,128)}, f32[512,512]{1,0:T(8,128)}) custom-call(bf16[64,2,16,128]{3,2,1,0:T(8,128)(2,1)S(1)} %bitcast.4, bf16[64,2,16,128]{3,2,1,0:T(8,128)(2,1)S(1)} %collective-permute-done.1.other_ref), custom_call_target="tpu_custom_call" | custom-call | flops 524288 | bytes 3145728 | tf_op jit(solution)/shard_map/lay_weights/pallas_call | solution.py:525
Async XLA Ops:
  5.1 42.0 %all-to-all-start = ((bf16[128,16,512]{2,1,0:T(8,128)(2,1)}), bf16[128,16,512]{2,1,0:T(8,128)(2,1)}, u32[]{:S(2)}, u32[]{:S(2)}) async-start(bf16[128,16,512]{2,1,0:T(8,128)(2,1)} %gather_rows.1), calls=%async_computation | async-start | bytes 4194304 | tf_op jit(solution)/shard_map/all_to_all | solution.py:558
  17.1 30.0 %copy-start = (bf16[1024,512]{1,0:T(8,128)(2,1)S(1)}, bf16[1024,512]{1,0:T(8,128)(2,1)}, u32[]{:S(2)}) copy-start(bf16[1024,512]{1,0:T(8,128)(2,1)} %feats_ref.3) | copy-start | bytes 3145732
  17.1 30.0 %copy-start.1 = (bf16[512,512]{1,0:T(8,128)(2,1)S(1)}, bf16[512,512]{1,0:T(8,128)(2,1)}, u32[]{:S(2)}) copy-start(bf16[512,512]{1,0:T(8,128)(2,1)} %wn_ref.3) | copy-start | bytes 1572868
  17.1 30.0 %copy-start.2 = (bf16[1024,512]{1,0:T(8,128)(2,1)S(1)}, bf16[1024,512]{1,0:T(8,128)(2,1)}, u32[]{:S(2)}) copy-start(bf16[1024,512]{1,0:T(8,128)(2,1)} %gout_ref.1) | copy-start | bytes 3145732
  55.0 2.7 %collective-permute-start = (bf16[64,2,16,128]{3,2,1,0:T(8,128)(2,1)S(1)}, bf16[64,2,16,128]{3,2,1,0:T(8,128)(2,1)S(1)}, u32[]{:S(2)}, u32[]{:S(2)}) collective-permute-start(bf16[64,2,16,128]{3,2,1,0:T(8,128)(2,1)S(1)} %get-tuple-element.27), channel_id=1, source_target_pairs={{0,1},{1,0},{2,3},{3,2},{4,5},{5,4},{6,7},{7,6},{8,9},{9,8},{10,11... | collective-permute-start | bytes 1572872 | tf_op jit(solution)/shard_map/ppermute | solution.py:571
  58.6 16.8 %all-to-all-start.1 = ((bf16[64,2,16,128]{3,2,1,0:T(8,128)(2,1)}), bf16[64,2,16,128]{3,2,1,0:T(8,128)(2,1)S(1)}, u32[]{:S(2)}, u32[]{:S(2)}) async-start(bf16[64,2,16,128]{3,2,1,0:T(8,128)(2,1)} %add_pair.1), calls=%async_computation.1 | async-start | bytes 1048576 | tf_op jit(solution)/shard_map/all_to_all | solution.py:558
  76.3 41.6 %all-to-all-start.2 = ((bf16[128,16,640]{2,1,0:T(8,128)(2,1)}), bf16[128,16,640]{2,1,0:T(8,128)(2,1)S(1)}, u32[]{:S(2)}, u32[]{:S(2)}) async-start(bf16[128,16,640]{2,1,0:T(8,128)(2,1)} %lay_shares.1), calls=%async_computation.2 | async-start | bytes 5242880 | tf_op jit(solution)/shard_map/all_to_all | solution.py:558
  86.7 32.5 %copy-start.3 = (s32[128,16]{0,1:T(8,128)S(1)}, s32[128,16]{0,1:T(8,128)}, u32[]{:S(2)}) copy-start(s32[128,16]{0,1:T(8,128)} %param.20) | copy-start | bytes 24580
  86.7 32.5 %copy-start.4 = (s32[1,128]{1,0:T(1,128)S(1)}, s32[1,128]{1,0:T(1,128)}, u32[]{:S(2)}) copy-start(s32[1,128]{1,0:T(1,128)} %cnt_ref.5) | copy-start | bytes 1540
  118.0 4.5 %collective-permute-start.1 = (bf16[64,2,16,128]{3,2,1,0:T(8,128)(2,1)S(1)}, bf16[64,2,16,128]{3,2,1,0:T(8,128)(2,1)S(1)}, u32[]{:S(2)}, u32[]{:S(2)}) collective-permute-start(bf16[64,2,16,128]{3,2,1,0:T(8,128)(2,1)S(1)} %bitcast.3), channel_id=1, source_target_pairs={{0,1},{1,0},{2,3},{3,2},{4,5},{5,4},{6,7},{7,6},{8,9},{9,8},{10,11... | collective-permute-start | bytes 1572872 | tf_op jit(solution)/shard_map/ppermute | solution.py:579

commit v2 on v1

--- a/solution.py
+++ b/solution.py
@@ -40,6 +40,9 @@
 LAYER_PARAMS = pltpu.CompilerParams(vmem_limit_bytes=48 * MIB)
 BACK_PARAMS = pltpu.CompilerParams(vmem_limit_bytes=56 * MIB)
 LAY_PARAMS = pltpu.CompilerParams(vmem_limit_bytes=52 * MIB)
+
+
+PLANES = 16
 
 
 def cost(macs, moved):
@@ -117,8 +120,8 @@
 
 
 def combine_kernel(
-    src_ref, cnt_ref, adj_ref, feats_ref, ws_ref, wn_ref,
-    cb_ref, cbt_ref, cot_ref, self_ref, own_ref, wst_ref, wnt_ref,
+    src_ref, cnt_ref, adj_ref, feats_ref, gout_ref, ws_ref, wn_ref,
+    cb_ref, cbt_ref, cot_ref, self_ref, own_ref, wst_ref, wnt_ref, late_ref,
     acc,
 ):
     i = pl.program_id(0)
@@ -130,6 +133,10 @@
     def _():
         wst_ref[...] = ws_ref[...].T
         wnt_ref[...] = wn_ref[...].T
+
+    late_ref[0] = gout_ref[...]
+    part = lax.rem(i, wn_ref.shape[0] // rows)
+    late_ref[1] = wn_ref[pl.ds(pl.multiple_of(part * rows, rows), rows), :]
 
     @pl.loop(0, cnt_ref[i])
     def _(j):
@@ -152,7 +159,7 @@
     self_ref[...] = dot(mine, ws_ref[...])
 
 
-def combine(tile_source_rows, tile_cnt, adj_tiles, feats, w_self, w_neigh, all_tiles):
+def combine(tile_source_rows, tile_cnt, adj_tiles, feats, grad_out, w_self, w_neigh, all_tiles):
     dst_tiles, slots, rows, _ = adj_tiles.shape
     nodes, width = feats.shape
     bnd = all_tiles * rows - nodes
@@ -164,6 +171,7 @@
         jax.ShapeDtypeStruct((nodes, width), F32),
         jax.ShapeDtypeStruct((width, width), BF16),
         jax.ShapeDtypeStruct((width, width), BF16),
+        jax.ShapeDtypeStruct((PLANES, nodes, width), BF16),
     ]
     return pl.pallas_call(
         combine_kernel,
@@ -174,6 +182,7 @@
             scalars(),
             pl.BlockSpec((1, slots, rows, rows), lambda i: (i, 0, 0, 0)),
             whole((nodes, width)),
+            pl.BlockSpec((rows, width), lambda i: (i, 0)),
             whole((width, width)),
             whole((width, width)),
         ],
@@ -185,12 +194,13 @@
             pl.BlockSpec((rows, width), lambda i: (i, 0)),
             whole((width, width)),
             whole((width, width)),
+            pl.BlockSpec((2, rows, width), lambda i: (0, i, 0)),
         ],
         scratch_shapes=[pltpu.VMEM((all_tiles, rows, rows), F32)],
         compiler_params=PARAMS,
         cost_estimate=cost(nodes * width * (nodes + width), 20 * MIB),
         name="combine_tiles",
-    )(tile_source_rows, tile_cnt, adj_tiles, feats, w_self, w_neigh)
+    )(tile_source_rows, tile_cnt, adj_tiles, feats, grad_out, w_self, w_neigh)
 
 
 class Stream:
@@ -211,24 +221,24 @@
 
 
 def layer_kernel(
-    cb_ref, in_ref, self_ref, own_ref, gout_ref, wn_ref, feats_ref,
+    cb_ref, in_ref, self_ref, own_ref, late_ref, feats_ref,
     act_ref, gpre_ref, keep_ref, pass_ref,
-    cb, rows_in, self_pre, own, gout, wn, feats, left, act, gpre, keep, give,
-    cb_sems, in_sems, sems, out_sems,
+    cb, self_pre, own, gout, wn, feats, left, act, gpre, keep, give,
+    cb_sems, sems, out_sems,
 ):
-    bnd, width = rows_in.shape
+    bnd, width = in_ref.shape
     cuts = [0, bnd // 8, bnd // 4, bnd // 2, 3 * bnd // 4, bnd]
     cuts = list(zip(cuts[:-1], cuts[1:]))
     spans = [pl.ds(a, b - a) for a, b in cuts]
     copy = pltpu.make_async_copy
     get_cb = [copy(cb_ref.at[:, d], cb.at[:, d], cb_sems.at[k]) for k, d in enumerate(spans)]
-    get_in = [copy(in_ref.at[d], rows_in.at[d], in_sems.at[k]) for k, d in enumerate(spans)]
     rest = [
-        (own_ref, own), (wn_ref, wn), (self_ref, self_pre), (gout_ref, gout),
+        (own_ref, own), (late_ref.at[1, pl.ds(0, width)], wn), (self_ref, self_pre),
+        (late_ref.at[0], gout),
         (feats_ref, feats),
     ]
     rest = [copy(src, dst, sems.at[n]) for n, (src, dst) in enumerate(rest)]
-    loads = Stream([c for pair in zip(get_cb, get_in) for c in pair] + rest, 6)
+    loads = Stream(get_cb + rest, 5)
     outs = []
 
     def put(src, dst):
@@ -237,8 +247,8 @@
 
     total = None
     for k, (a, b) in enumerate(cuts):
-        loads.wait(get_cb[k], get_in[k])
-        term = dot(cb[:, a:b], rows_in[a:b, :])
+        loads.wait(get_cb[k])
+        term = dot(cb[:, a:b], in_ref[a:b, :])
         total = term if total is None else total + term
     loads.wait(rest[0])
     agg = (total + own[...]).astype(BF16)
@@ -272,10 +282,7 @@
         c.wait()
 
 
-PLANES = 16
-
-
-def layer(cb, incoming, self_pre, own_agg, grad_out, w_neigh, feats, chips):
+def layer(cb, incoming, self_pre, own_agg, late, feats, chips):
     nodes, bnd = cb.shape
     width = incoming.shape[1]
     chunks = 5
@@ -290,11 +297,10 @@
             jax.ShapeDtypeStruct(shares, F32),
             jax.ShapeDtypeStruct(shares, BF16),
         ],
-        in_specs=[anywhere()] * 7,
+        in_specs=[anywhere(), in_vmem()] + [anywhere()] * 4,
         out_specs=[anywhere()] * 4,
         scratch_shapes=[
             vmem((nodes, bnd), BF16),
-            vmem((bnd, width), BF16),
             vmem((nodes, width), F32),
             vmem((nodes, width), F32),
             vmem((nodes, width), BF16),
@@ -306,14 +312,13 @@
             vmem(shares, F32),
             vmem(shares, BF16),
             sems((chunks,)),
-            sems((chunks,)),
             sems((5,)),
             sems((4,)),
         ],
         compiler_params=LAYER_PARAMS,
         cost_estimate=cost(nodes * width * (bnd + 3 * width), 18 * MIB),
         name="layer",
-    )(cb, incoming, self_pre, own_agg, grad_out, w_neigh, feats)
+    )(cb, incoming, self_pre, own_agg, late, feats)
 
 
 def boundary_kernel(
@@ -562,11 +567,11 @@
     slot_rows = send_idx.T
     outgoing = gather(slot_rows, send_cnt, stale_feats)
     incoming = exchange(outgoing, None).reshape(peers * slots, width)
-    cb, cbt, cot, self_pre, own_agg, w_self_t, w_neigh_t = combine(
-        tile_source_rows, tile_cnt, adj_tiles, feats, w_self, w_neigh, all_tiles
+    cb, cbt, cot, self_pre, own_agg, w_self_t, w_neigh_t, late = combine(
+        tile_source_rows, tile_cnt, adj_tiles, feats, grad_out, w_self, w_neigh, all_tiles
     )
     activated, grad_pre, keep, give = layer(
-        cb, incoming, self_pre, own_agg, grad_out, w_neigh, feats, chips
+        cb, incoming, self_pre, own_agg, late, feats, chips
     )
     got = lax.ppermute(give, "dom", pairs)
     parts = exchange(add_pair(keep, got), same_core)

time: 125 us -> 124 us (level)
  no operation moved by 1% of the time
where the time goes in v2:
time: 124 us
  waiting for transfers between devices  57.1 us (46%)
  Pallas kernels  42 us (34%)
  starting transfers between devices  23.8 us (19%)
    all_to_all x3, waiting for transfers between devices, exchange(): lax.all_to_all(v, 'dom', split_axis=0, concat_axis=0, tiled=True, axis_in...  55.5 us
    all_to_all x3, starting transfers between devices, exchange(): lax.all_to_all(v, 'dom', split_axis=0, concat_axis=0, tiled=True, axis_in...  21.5 us
    pallas_call x1, Pallas kernels, combine(): pl.pallas_call(combine_kernel, grid=(dst_tiles,), out_shape=out_shape, in...  12.1 us
    pallas_call x1, Pallas kernels, layer(): pl.pallas_call(layer_kernel, out_shape=[jax.ShapeDtypeStruct((nodes, widt...  7.5 us
    pallas_call x1, Pallas kernels, boundary(): pl.pallas_call(boundary_kernel, out_shape=[jax.ShapeDtypeStruct((peers, s...  6.14 us
    pallas_call x1, Pallas kernels, feats_grad(): pl.pallas_call(feats_grad_kernel, grid=(nodes // block,), out_shape=jax.S...  4.95 us
    pallas_call x1, Pallas kernels, gather(): pl.pallas_call(gather_kernel, out_shape=jax.ShapeDtypeStruct((peers, slot...  4.47 us
    pallas_call x1, Pallas kernels, scatter(): pl.pallas_call(functools.partial(scatter_kernel, chunks=chunks), out_shap...  3.35 us
  transfers between devices with their start and end apart: 5, of which 4 were waited for; matrix products, arithmetic and copies ran while one was open for 0% of the time, Pallas kernels for 21%

profile of v2, /device:TPU:1, one launch (start us, length us, event | category | flops | bytes accessed | tf_op | source)
XLA Modules:
  0.0 123.6 jit_solution(1079705284348105073)
XLA Ops:
  0.6 4.5 %gather_rows.1 = bf16[128,16,512]{2,1,0:T(8,128)(2,1)} custom-call(s32[16,128]{1,0:T(8,128)} %bitcast.6, s32[1,128]{1,0:T(1,128)} %cnt_ref.5, bf16[1024,512]{1,0:T(8,128)(2,1)} %rows_ref.1), custom_call_target="tpu_custom_call" | custom-call | flops 2147483648 | bytes 3145728 | tf_op jit(solution)/shard_map/gather_rows/pallas_call | solution.py:103
  5.1 11.5 %all-to-all-start = ((bf16[128,16,512]{2,1,0:T(8,128)(2,1)}), bf16[128,16,512]{2,1,0:T(8,128)(2,1)S(1)}, u32[]{:S(2)}, u32[]{:S(2)}) async-start(bf16[128,16,512]{2,1,0:T(8,128)(2,1)} %gather_rows.1), calls=%async_computation | async-start | bytes 4194304 | tf_op jit(solution)/shard_map/all_to_all | solution.py:563
  16.6 0.0 copy-start
  16.6 12.1 %combine_tiles.1 = (bf16[1024,2048]{1,0:T(8,128)(2,1)}, bf16[2048,1024]{1,0:T(8,128)(2,1)}, bf16[1024,1024]{1,0:T(8,128)(2,1)}, f32[1024,512]{1,0:T(8,128)}, f32...) custom-call(s32[8,16]{1,0:T(8,128)} %src_ref.1, ...), custom_call_target="tpu_custom_call" | custom-call | flops 1610612736 | bytes 20971520 | tf_op jit(solution)/shard_map/combine_tiles/pallas_call | solution.py:176
  28.7 18.3 %all-to-all-done = bf16[128,16,512]{2,1,0:T(8,128)(2,1)S(1)} async-done(((bf16[128,16,512]{2,1,0:T(8,128)(2,1)}), bf16[128,16,512]{2,1,0:T(8,128)(2,1)S(1)}, u32[]{:S(2)}, u32[]{:S(2)}) %all-to-all-start) | async-done | bytes 2097184 | tf_op jit(solution)/shard_map/all_to_all | solution.py:563
  47.0 0.0 copy-done
  47.0 7.5 %layer.1 = (bf16[1024,512]{1,0:T(8,128)(2,1)}, bf16[16,1024,512]{2,1,0:T(8,128)(2,1)}, f32[64,2,16,128]{3,2,1,0:T(8,128)S(1)}, bf16[64,2,16,128]{3,2,1,0:T(8,128)(2,1)S(1)}) custom-call(bf16[1024,2048]{1,0:T(8,128)(2,1)} %get-tuple-element.23.cb_ref, bf16[2048,512]{1,0:T(8,128)(2,1)S(1)} %bitcast.3, f32[1024,512]{1,0:T(8,128)} %get-tuple-element.24.self_ref, ...), custom_call_target="tpu_custom_call" | custom-call | flops 3758096384 | bytes 18874368 | tf_op jit(solution)/shard_map/layer/pallas_call | solution.py:292
  54.5 1.2 collective-permute-start
  55.7 1.5 %collective-permute-done.got_ref = bf16[64,2,16,128]{3,2,1,0:T(8,128)(2,1)S(1)} collective-permute-done((bf16[64,2,16,128]{3,2,1,0:T(8,128)(2,1)S(1)}, bf16[64,2,16,128]{3,2,1,0:T(8,128)(2,1)S(1)}, u32[]{:S(2)}, u32[]{:S(2)}) %collective-permute-start) | collective-permute-done | bytes 524320 | tf_op jit(solution)/shard_map/ppermute | solution.py:576
  57.2 0.9 add_pair.1
  58.1 4.6 %all-to-all-start.1 = ((bf16[64,2,16,128]{3,2,1,0:T(8,128)(2,1)}), bf16[64,2,16,128]{3,2,1,0:T(8,128)(2,1)S(1)}, u32[]{:S(2)}, u32[]{:S(2)}) async-start(bf16[64,2,16,128]{3,2,1,0:T(8,128)(2,1)} %add_pair.1), calls=%async_computation.1 | async-start | bytes 1048576 | tf_op jit(solution)/shard_map/all_to_all | solution.py:563
  62.8 6.1 %boundary_grads.1 = (bf16[128,16,640]{2,1,0:T(8,128)(2,1)}, bf16[1024,512]{1,0:T(8,128)(2,1)}) custom-call(bf16[2048,1024]{1,0:T(8,128)(2,1)} %get-tuple-element.30.cbt_ref, bf16[16,1024,512]{2,1,0:T(8,128)(2,1)} %get-tuple-element.31.gpre_ref, bf16[512,512]{1,0:T(8,128)(2,1)} %get-tuple-element.32.wnt_ref), custom_call_target="tpu_custom_call" | custom-call | flops 2684354560 | bytes 9437184 | tf_op jit(solution)/shard_map/boundary_grads/pallas_call | solution.py:364
  68.9 6.0 %all-to-all-done.1.parts_ref = bf16[64,2,16,128]{3,2,1,0:T(8,128)(2,1)S(1)} async-done(((bf16[64,2,16,128]{3,2,1,0:T(8,128)(2,1)}), bf16[64,2,16,128]{3,2,1,0:T(8,128)(2,1)S(1)}, u32[]{:S(2)}, u32[]{:S(2)}) %all-to-all-start.1) | async-done | bytes 524320 | tf_op jit(solution)/shard_map/all_to_all | solution.py:563
  74.9 1.0 lay_shares.1
  75.9 5.4 %all-to-all-start.2 = ((bf16[128,16,640]{2,1,0:T(8,128)(2,1)}), bf16[128,16,640]{2,1,0:T(8,128)(2,1)S(1)}, u32[]{:S(2)}, u32[]{:S(2)}) async-start(bf16[128,16,640]{2,1,0:T(8,128)(2,1)} %lay_shares.1), calls=%async_computation.2 | async-start | bytes 5242880 | tf_op jit(solution)/shard_map/all_to_all | solution.py:563
  81.3 5.0 %feats_grad.1 = bf16[1024,512]{1,0:T(8,128)(2,1)} custom-call(bf16[1024,1024]{1,0:T(8,128)(2,1)} %get-tuple-element.34.cot_ref, bf16[1024,512]{1,0:T(8,128)(2,1)} %get-tuple-element.35.gagg_ref, bf16[16,1024,512]{2,1,0:T(8,128)(2,1)} %get-tuple-element.31.gpre_ref, bf16[512,512]{1,0:T(8,128)(2,1)} %get-tuple-element.36.wst_ref, bf16[1024,512]{1,0:T(8,128)(2,1)} %stale_ref.1), custom_call_target="tpu_custom_call" | custom-call | flops 1610612736 | bytes 7340032 | tf_op jit(solution)/shard_map/feats_grad/pallas_call | solution.py:397
  86.3 0.0 copy-start.1
  86.3 0.0 copy-start.2
  86.3 31.2 %all-to-all-done.2.ret_ref = bf16[128,16,640]{2,1,0:T(8,128)(2,1)S(1)} async-done(((bf16[128,16,640]{2,1,0:T(8,128)(2,1)}), bf16[128,16,640]{2,1,0:T(8,128)(2,1)S(1)}, u32[]{:S(2)}, u32[]{:S(2)}) %all-to-all-start.2) | async-done | bytes 2621472 | tf_op jit(solution)/shard_map/all_to_all | solution.py:563
  117.5 0.1 take_shares.1
  117.6 1.1 collective-permute-start.1
  118.7 0.0 copy-done.1
  118.7 0.0 copy-done.2
  118.7 3.3 %scatter_rows.1 = bf16[1024,512]{1,0:T(8,128)(2,1)} custom-call(s32[16,128]{1,0:T(8,128)S(1)} %bitcast.7, s32[1,128]{1,0:T(1,128)S(1)} %copy-done.2, bf16[128,16,640]{2,1,0:T(8,128)(2,1)S(1)} %all-to-all-done.2.ret_ref), custom_call_target="tpu_custom_call" | custom-call | flops 2684354560 | bytes 4194304 | tf_op jit(solution)/shard_map/scatter_rows/pallas_call | solution.py:506
  122.1 0.0 collective-permute-done.1.other_ref
  122.1 1.5 %lay_weights.1 = (f32[512,512]{1,0:T(8,128)}, f32[512,512]{1,0:T(8,128)}) custom-call(bf16[64,2,16,128]{3,2,1,0:T(8,128)(2,1)S(1)} %bitcast.5, bf16[64,2,16,128]{3,2,1,0:T(8,128)(2,1)S(1)} %collective-permute-done.1.other_ref), custom_call_target="tpu_custom_call" | custom-call | flops 524288 | bytes 3145728 | tf_op jit(solution)/shard_map/lay_weights/pallas_call | solution.py:530
Async XLA Ops:
  5.1 41.9 %all-to-all-start = ((bf16[128,16,512]{2,1,0:T(8,128)(2,1)}), bf16[128,16,512]{2,1,0:T(8,128)(2,1)S(1)}, u32[]{:S(2)}, u32[]{:S(2)}) async-start(bf16[128,16,512]{2,1,0:T(8,128)(2,1)} %gather_rows.1), calls=%async_computation | async-start | bytes 4194304 | tf_op jit(solution)/shard_map/all_to_all | solution.py:563
  16.6 30.4 %copy-start = (bf16[1024,512]{1,0:T(8,128)(2,1)S(1)}, bf16[1024,512]{1,0:T(8,128)(2,1)}, u32[]{:S(2)}) copy-start(bf16[1024,512]{1,0:T(8,128)(2,1)} %feats_ref.3) | copy-start | bytes 3145732
  54.5 2.7 %collective-permute-start = (bf16[64,2,16,128]{3,2,1,0:T(8,128)(2,1)S(1)}, bf16[64,2,16,128]{3,2,1,0:T(8,128)(2,1)S(1)}, u32[]{:S(2)}, u32[]{:S(2)}) collective-permute-start(bf16[64,2,16,128]{3,2,1,0:T(8,128)(2,1)S(1)} %get-tuple-element.29), channel_id=1, source_target_pairs={{0,1},{1,0},{2,3},{3,2},{4,5},{5,4},{6,7},{7,6},{8,9},{9,8},{10,11... | collective-permute-start | bytes 1572872 | tf_op jit(solution)/shard_map/ppermute | solution.py:576
  58.1 16.8 %all-to-all-start.1 = ((bf16[64,2,16,128]{3,2,1,0:T(8,128)(2,1)}), bf16[64,2,16,128]{3,2,1,0:T(8,128)(2,1)S(1)}, u32[]{:S(2)}, u32[]{:S(2)}) async-start(bf16[64,2,16,128]{3,2,1,0:T(8,128)(2,1)} %add_pair.1), calls=%async_computation.1 | async-start | bytes 1048576 | tf_op jit(solution)/shard_map/all_to_all | solution.py:563
  75.9 41.6 %all-to-all-start.2 = ((bf16[128,16,640]{2,1,0:T(8,128)(2,1)}), bf16[128,16,640]{2,1,0:T(8,128)(2,1)S(1)}, u32[]{:S(2)}, u32[]{:S(2)}) async-start(bf16[128,16,640]{2,1,0:T(8,128)(2,1)} %lay_shares.1), calls=%async_computation.2 | async-start | bytes 5242880 | tf_op jit(solution)/shard_map/all_to_all | solution.py:563
  86.3 32.5 %copy-start.1 = (s32[128,16]{0,1:T(8,128)S(1)}, s32[128,16]{0,1:T(8,128)}, u32[]{:S(2)}) copy-start(s32[128,16]{0,1:T(8,128)} %param.20) | copy-start | bytes 24580
  86.3 32.5 %copy-start.2 = (s32[1,128]{1,0:T(1,128)S(1)}, s32[1,128]{1,0:T(1,128)}, u32[]{:S(2)}) copy-start(s32[1,128]{1,0:T(1,128)} %cnt_ref.5) | copy-start | bytes 1540
  117.6 4.5 %collective-permute-start.1 = (bf16[64,2,16,128]{3,2,1,0:T(8,128)(2,1)S(1)}, bf16[64,2,16,128]{3,2,1,0:T(8,128)(2,1)S(1)}, u32[]{:S(2)}, u32[]{:S(2)}) collective-permute-start(bf16[64,2,16,128]{3,2,1,0:T(8,128)(2,1)S(1)} %bitcast.4), channel_id=1, source_target_pairs={{0,1},{1,0},{2,3},{3,2},{4,5},{5,4},{6,7},{7,6},{8,9},{9,8},{10,11... | collective-permute-start | bytes 1572872 | tf_op jit(solution)/shard_map/ppermute | solution.py:584

commit v3 on v2

--- a/solution.py
+++ b/solution.py
@@ -37,7 +37,7 @@
 
 SMALL_PARAMS = pltpu.CompilerParams(vmem_limit_bytes=16 * MIB)
 PARAMS = pltpu.CompilerParams(vmem_limit_bytes=56 * MIB)
-LAYER_PARAMS = pltpu.CompilerParams(vmem_limit_bytes=48 * MIB)
+LAYER_PARAMS = pltpu.CompilerParams(vmem_limit_bytes=50 * MIB)
 BACK_PARAMS = pltpu.CompilerParams(vmem_limit_bytes=56 * MIB)
 LAY_PARAMS = pltpu.CompilerParams(vmem_limit_bytes=52 * MIB)
 
@@ -121,7 +121,7 @@
 
 def combine_kernel(
     src_ref, cnt_ref, adj_ref, feats_ref, gout_ref, ws_ref, wn_ref,
-    cb_ref, cbt_ref, cot_ref, self_ref, own_ref, wst_ref, wnt_ref, late_ref,
+    cb_ref, cbt_ref, cot_ref, self_ref, own_ref, wst_ref, wnt_ref, late_ref, ft_ref,
     acc,
 ):
     i = pl.program_id(0)
@@ -157,6 +157,7 @@
     own_ref[...] = dot(jnp.concatenate(own, axis=1), feats)
     mine = feats_ref[pl.ds(pl.multiple_of(i * rows, rows), rows), :]
     self_ref[...] = dot(mine, ws_ref[...])
+    ft_ref[0] = mine.T
 
 
 def combine(tile_source_rows, tile_cnt, adj_tiles, feats, grad_out, w_self, w_neigh, all_tiles):
@@ -172,6 +173,7 @@
         jax.ShapeDtypeStruct((width, width), BF16),
         jax.ShapeDtypeStruct((width, width), BF16),
         jax.ShapeDtypeStruct((PLANES, nodes, width), BF16),
+        jax.ShapeDtypeStruct((PLANES, width, nodes), BF16),
     ]
     return pl.pallas_call(
         combine_kernel,
@@ -195,6 +197,7 @@
             whole((width, width)),
             whole((width, width)),
             pl.BlockSpec((2, rows, width), lambda i: (0, i, 0)),
+            pl.BlockSpec((1, width, rows), lambda i: (0, 0, i)),
         ],
         scratch_shapes=[pltpu.VMEM((all_tiles, rows, rows), F32)],
         compiler_params=PARAMS,
@@ -221,9 +224,9 @@
 
 
 def layer_kernel(
-    cb_ref, in_ref, self_ref, own_ref, late_ref, feats_ref,
+    cb_ref, in_ref, self_ref, own_ref, late_ref, ft_ref,
     act_ref, gpre_ref, keep_ref, pass_ref,
-    cb, self_pre, own, gout, wn, feats, left, act, gpre, keep, give,
+    cb, self_pre, own, gout, wn, left, act, gpre, keep, give,
     cb_sems, sems, out_sems,
 ):
     bnd, width = in_ref.shape
@@ -235,7 +238,7 @@
     rest = [
         (own_ref, own), (late_ref.at[1, pl.ds(0, width)], wn), (self_ref, self_pre),
         (late_ref.at[0], gout),
-        (feats_ref, feats),
+        (ft_ref.at[0], left.at[pl.ds(0, width)]),
     ]
     rest = [copy(src, dst, sems.at[n]) for n, (src, dst) in enumerate(rest)]
     loads = Stream(get_cb + rest, 5)
@@ -267,7 +270,6 @@
     put(act, act_ref)
     put(gpre, gpre_ref.at[0])
     loads.wait(rest[4])
-    left[:width, :] = feats[...].T
     first = first_core()
     groups, halves, rows, lanes = keep.shape
     g = dot(left[...], gpre[...]).reshape(groups, rows, width)
@@ -282,7 +284,7 @@
         c.wait()
 
 
-def layer(cb, incoming, self_pre, own_agg, late, feats, chips):
+def layer(cb, incoming, self_pre, own_agg, late, feats_t, chips):
     nodes, bnd = cb.shape
     width = incoming.shape[1]
     chunks = 5
@@ -305,7 +307,6 @@
             vmem((nodes, width), F32),
             vmem((nodes, width), BF16),
             vmem((width, width), BF16),
-            vmem((nodes, width), BF16),
             vmem((2 * width, nodes), BF16),
             vmem((nodes, width), BF16),
             vmem((nodes, width), BF16),
@@ -318,7 +319,7 @@
         compiler_params=LAYER_PARAMS,
         cost_estimate=cost(nodes * width * (bnd + 3 * width), 18 * MIB),
         name="layer",
-    )(cb, incoming, self_pre, own_agg, late, feats)
+    )(cb, incoming, self_pre, own_agg, late, feats_t)
 
 
 def boundary_kernel(
@@ -567,11 +568,11 @@
     slot_rows = send_idx.T
     outgoing = gather(slot_rows, send_cnt, stale_feats)
     incoming = exchange(outgoing, None).reshape(peers * slots, width)
-    cb, cbt, cot, self_pre, own_agg, w_self_t, w_neigh_t, late = combine(
+    cb, cbt, cot, self_pre, own_agg, w_self_t, w_neigh_t, late, feats_t = combine(
         tile_source_rows, tile_cnt, adj_tiles, feats, grad_out, w_self, w_neigh, all_tiles
     )
     activated, grad_pre, keep, give = layer(
-        cb, incoming, self_pre, own_agg, late, feats, chips
+        cb, incoming, self_pre, own_agg, late, feats_t, chips
     )
     got = lax.ppermute(give, "dom", pairs)
     parts = exchange(add_pair(keep, got), same_core)

time: 124 us -> 124 us (level)
  no operation moved by 1% of the time
where the time goes in v3:
time: 124 us
  waiting for transfers between devices  57.2 us (46%)
  Pallas kernels  41.8 us (34%)
  starting transfers between devices  23.8 us (19%)
    all_to_all x3, waiting for transfers between devices, exchange(): lax.all_to_all(v, 'dom', split_axis=0, concat_axis=0, tiled=True, axis_in...  55.6 us
    all_to_all x3, starting transfers between devices, exchange(): lax.all_to_all(v, 'dom', split_axis=0, concat_axis=0, tiled=True, axis_in...  21.5 us
    pallas_call x1, Pallas kernels, combine(): pl.pallas_call(combine_kernel, grid=(dst_tiles,), out_shape=out_shape, in...  12 us
    pallas_call x1, Pallas kernels, layer(): pl.pallas_call(layer_kernel, out_shape=[jax.ShapeDtypeStruct((nodes, widt...  7.44 us
    pallas_call x1, Pallas kernels, boundary(): pl.pallas_call(boundary_kernel, out_shape=[jax.ShapeDtypeStruct((peers, s...  6.18 us
    pallas_call x1, Pallas kernels, feats_grad(): pl.pallas_call(feats_grad_kernel, grid=(nodes // block,), out_shape=jax.S...  4.95 us
    pallas_call x1, Pallas kernels, gather(): pl.pallas_call(gather_kernel, out_shape=jax.ShapeDtypeStruct((peers, slot...  4.47 us
    pallas_call x1, Pallas kernels, scatter(): pl.pallas_call(functools.partial(scatter_kernel, chunks=chunks), out_shap...  3.35 us
  transfers between devices with their start and end apart: 5, of which 4 were waited for; matrix products, arithmetic and copies ran while one was open for 0% of the time, Pallas kernels for 21%

profile of v3, /device:TPU:1, one launch (start us, length us, event | category | flops | bytes accessed | tf_op | source)
XLA Modules:
  0.0 123.5 jit_solution(15736984689087207098)
XLA Ops:
  0.6 4.5 %gather_rows.1 = bf16[128,16,512]{2,1,0:T(8,128)(2,1)} custom-call(s32[16,128]{1,0:T(8,128)} %bitcast.6, s32[1,128]{1,0:T(1,128)} %cnt_ref.5, bf16[1024,512]{1,0:T(8,128)(2,1)} %rows_ref.1), custom_call_target="tpu_custom_call" | custom-call | flops 2147483648 | bytes 3145728 | tf_op jit(solution)/shard_map/gather_rows/pallas_call | solution.py:103
  5.1 11.5 %all-to-all-start = ((bf16[128,16,512]{2,1,0:T(8,128)(2,1)}), bf16[128,16,512]{2,1,0:T(8,128)(2,1)S(1)}, u32[]{:S(2)}, u32[]{:S(2)}) async-start(bf16[128,16,512]{2,1,0:T(8,128)(2,1)} %gather_rows.1), calls=%async_computation | async-start | bytes 4194304 | tf_op jit(solution)/shard_map/all_to_all | solution.py:564
  16.6 12.0 %combine_tiles.1 = (bf16[1024,2048]{1,0:T(8,128)(2,1)}, bf16[2048,1024]{1,0:T(8,128)(2,1)}, bf16[1024,1024]{1,0:T(8,128)(2,1)}, f32[1024,512]{1,0:T(8,128)}, f32...) custom-call(s32[8,16]{1,0:T(8,128)} %src_ref.1, ...), custom_call_target="tpu_custom_call" | custom-call | flops 1610612736 | bytes 20971520 | tf_op jit(solution)/shard_map/combine_tiles/pallas_call | solution.py:178
  28.6 18.4 %all-to-all-done = bf16[128,16,512]{2,1,0:T(8,128)(2,1)S(1)} async-done(((bf16[128,16,512]{2,1,0:T(8,128)(2,1)}), bf16[128,16,512]{2,1,0:T(8,128)(2,1)S(1)}, u32[]{:S(2)}, u32[]{:S(2)}) %all-to-all-start) | async-done | bytes 2097184 | tf_op jit(solution)/shard_map/all_to_all | solution.py:564
  47.0 7.4 %layer.1 = (bf16[1024,512]{1,0:T(8,128)(2,1)}, bf16[16,1024,512]{2,1,0:T(8,128)(2,1)}, f32[64,2,16,128]{3,2,1,0:T(8,128)S(1)}, bf16[64,2,16,128]{3,2,1,0:T(8,128)(2,1)S(1)}) custom-call(bf16[1024,2048]{1,0:T(8,128)(2,1)} %get-tuple-element.24.cb_ref, bf16[2048,512]{1,0:T(8,128)(2,1)S(1)} %bitcast.3, f32[1024,512]{1,0:T(8,128)} %get-tuple-element.25.self_ref, ...), custom_call_target="tpu_custom_call" | custom-call | flops 3758096384 | bytes 18874368 | tf_op jit(solution)/shard_map/layer/pallas_call | solution.py:294
  54.5 1.2 collective-permute-start
  55.7 1.5 %collective-permute-done.got_ref = bf16[64,2,16,128]{3,2,1,0:T(8,128)(2,1)S(1)} collective-permute-done((bf16[64,2,16,128]{3,2,1,0:T(8,128)(2,1)S(1)}, bf16[64,2,16,128]{3,2,1,0:T(8,128)(2,1)S(1)}, u32[]{:S(2)}, u32[]{:S(2)}) %collective-permute-start) | collective-permute-done | bytes 524320 | tf_op jit(solution)/shard_map/ppermute | solution.py:577
  57.2 0.9 add_pair.1
  58.1 4.6 %all-to-all-start.1 = ((bf16[64,2,16,128]{3,2,1,0:T(8,128)(2,1)}), bf16[64,2,16,128]{3,2,1,0:T(8,128)(2,1)S(1)}, u32[]{:S(2)}, u32[]{:S(2)}) async-start(bf16[64,2,16,128]{3,2,1,0:T(8,128)(2,1)} %add_pair.1), calls=%async_computation.1 | async-start | bytes 1048576 | tf_op jit(solution)/shard_map/all_to_all | solution.py:564
  62.7 6.2 %boundary_grads.1 = (bf16[128,16,640]{2,1,0:T(8,128)(2,1)}, bf16[1024,512]{1,0:T(8,128)(2,1)}) custom-call(bf16[2048,1024]{1,0:T(8,128)(2,1)} %get-tuple-element.32.cbt_ref, bf16[16,1024,512]{2,1,0:T(8,128)(2,1)} %get-tuple-element.33.gpre_ref, bf16[512,512]{1,0:T(8,128)(2,1)} %get-tuple-element.34.wnt_ref), custom_call_target="tpu_custom_call" | custom-call | flops 2684354560 | bytes 9437184 | tf_op jit(solution)/shard_map/boundary_grads/pallas_call | solution.py:365
  68.9 6.0 %all-to-all-done.1.parts_ref = bf16[64,2,16,128]{3,2,1,0:T(8,128)(2,1)S(1)} async-done(((bf16[64,2,16,128]{3,2,1,0:T(8,128)(2,1)}), bf16[64,2,16,128]{3,2,1,0:T(8,128)(2,1)S(1)}, u32[]{:S(2)}, u32[]{:S(2)}) %all-to-all-start.1) | async-done | bytes 524320 | tf_op jit(solution)/shard_map/all_to_all | solution.py:564
  74.9 1.0 lay_shares.1
  75.9 5.4 %all-to-all-start.2 = ((bf16[128,16,640]{2,1,0:T(8,128)(2,1)}), bf16[128,16,640]{2,1,0:T(8,128)(2,1)S(1)}, u32[]{:S(2)}, u32[]{:S(2)}) async-start(bf16[128,16,640]{2,1,0:T(8,128)(2,1)} %lay_shares.1), calls=%async_computation.2 | async-start | bytes 5242880 | tf_op jit(solution)/shard_map/all_to_all | solution.py:564
  81.2 5.0 %feats_grad.1 = bf16[1024,512]{1,0:T(8,128)(2,1)} custom-call(bf16[1024,1024]{1,0:T(8,128)(2,1)} %get-tuple-element.36.cot_ref, bf16[1024,512]{1,0:T(8,128)(2,1)} %get-tuple-element.37.gagg_ref, bf16[16,1024,512]{2,1,0:T(8,128)(2,1)} %get-tuple-element.33.gpre_ref, bf16[512,512]{1,0:T(8,128)(2,1)} %get-tuple-element.38.wst_ref, bf16[1024,512]{1,0:T(8,128)(2,1)} %stale_ref.1), custom_call_target="tpu_custom_call" | custom-call | flops 1610612736 | bytes 7340032 | tf_op jit(solution)/shard_map/feats_grad/pallas_call | solution.py:398
  86.2 0.0 copy-start
  86.2 0.0 copy-start.1
  86.2 31.2 %all-to-all-done.2.ret_ref = bf16[128,16,640]{2,1,0:T(8,128)(2,1)S(1)} async-done(((bf16[128,16,640]{2,1,0:T(8,128)(2,1)}), bf16[128,16,640]{2,1,0:T(8,128)(2,1)S(1)}, u32[]{:S(2)}, u32[]{:S(2)}) %all-to-all-start.2) | async-done | bytes 2621472 | tf_op jit(solution)/shard_map/all_to_all | solution.py:564
  117.5 0.1 take_shares.1
  117.5 1.1 collective-permute-start.1
  118.7 0.0 copy-done
  118.7 0.0 copy-done.1
  118.7 3.4 %scatter_rows.1 = bf16[1024,512]{1,0:T(8,128)(2,1)} custom-call(s32[16,128]{1,0:T(8,128)S(1)} %bitcast.7, s32[1,128]{1,0:T(1,128)S(1)} %copy-done.1, bf16[128,16,640]{2,1,0:T(8,128)(2,1)S(1)} %all-to-all-done.2.ret_ref), custom_call_target="tpu_custom_call" | custom-call | flops 2684354560 | bytes 4194304 | tf_op jit(solution)/shard_map/scatter_rows/pallas_call | solution.py:507
  122.0 0.0 collective-permute-done.1.other_ref
  122.0 1.5 %lay_weights.1 = (f32[512,512]{1,0:T(8,128)}, f32[512,512]{1,0:T(8,128)}) custom-call(bf16[64,2,16,128]{3,2,1,0:T(8,128)(2,1)S(1)} %bitcast.5, bf16[64,2,16,128]{3,2,1,0:T(8,128)(2,1)S(1)} %collective-permute-done.1.other_ref), custom_call_target="tpu_custom_call" | custom-call | flops 524288 | bytes 3145728 | tf_op jit(solution)/shard_map/lay_weights/pallas_call | solution.py:531
Async XLA Ops:
  5.1 41.9 %all-to-all-start = ((bf16[128,16,512]{2,1,0:T(8,128)(2,1)}), bf16[128,16,512]{2,1,0:T(8,128)(2,1)S(1)}, u32[]{:S(2)}, u32[]{:S(2)}) async-start(bf16[128,16,512]{2,1,0:T(8,128)(2,1)} %gather_rows.1), calls=%async_computation | async-start | bytes 4194304 | tf_op jit(solution)/shard_map/all_to_all | solution.py:564
  54.5 2.7 %collective-permute-start = (bf16[64,2,16,128]{3,2,1,0:T(8,128)(2,1)S(1)}, bf16[64,2,16,128]{3,2,1,0:T(8,128)(2,1)S(1)}, u32[]{:S(2)}, u32[]{:S(2)}) collective-permute-start(bf16[64,2,16,128]{3,2,1,0:T(8,128)(2,1)S(1)} %get-tuple-element.31), channel_id=1, source_target_pairs={{0,1},{1,0},{2,3},{3,2},{4,5},{5,4},{6,7},{7,6},{8,9},{9,8},{10,11... | collective-permute-start | bytes 1572872 | tf_op jit(solution)/shard_map/ppermute | solution.py:577
  58.1 16.8 %all-to-all-start.1 = ((bf16[64,2,16,128]{3,2,1,0:T(8,128)(2,1)}), bf16[64,2,16,128]{3,2,1,0:T(8,128)(2,1)S(1)}, u32[]{:S(2)}, u32[]{:S(2)}) async-start(bf16[64,2,16,128]{3,2,1,0:T(8,128)(2,1)} %add_pair.1), calls=%async_computation.1 | async-start | bytes 1048576 | tf_op jit(solution)/shard_map/all_to_all | solution.py:564
  75.9 41.6 %all-to-all-start.2 = ((bf16[128,16,640]{2,1,0:T(8,128)(2,1)}), bf16[128,16,640]{2,1,0:T(8,128)(2,1)S(1)}, u32[]{:S(2)}, u32[]{:S(2)}) async-start(bf16[128,16,640]{2,1,0:T(8,128)(2,1)} %lay_shares.1), calls=%async_computation.2 | async-start | bytes 5242880 | tf_op jit(solution)/shard_map/all_to_all | solution.py:564
  86.2 32.5 %copy-start = (s32[128,16]{0,1:T(8,128)S(1)}, s32[128,16]{0,1:T(8,128)}, u32[]{:S(2)}) copy-start(s32[128,16]{0,1:T(8,128)} %param.20) | copy-start | bytes 24580
  86.2 32.5 %copy-start.1 = (s32[1,128]{1,0:T(1,128)S(1)}, s32[1,128]{1,0:T(1,128)}, u32[]{:S(2)}) copy-start(s32[1,128]{1,0:T(1,128)} %cnt_ref.5) | copy-start | bytes 1540
  117.5 4.5 %collective-permute-start.1 = (bf16[64,2,16,128]{3,2,1,0:T(8,128)(2,1)S(1)}, bf16[64,2,16,128]{3,2,1,0:T(8,128)(2,1)S(1)}, u32[]{:S(2)}, u32[]{:S(2)}) collective-permute-start(bf16[64,2,16,128]{3,2,1,0:T(8,128)(2,1)S(1)} %bitcast.4), channel_id=1, source_target_pairs={{0,1},{1,0},{2,3},{3,2},{4,5},{5,4},{6,7},{7,6},{8,9},{9,8},{10,11... | collective-permute-start | bytes 1572872 | tf_op jit(solution)/shard_map/ppermute | solution.py:585

commit v4 on v3

--- a/solution.py
+++ b/solution.py
@@ -241,7 +241,7 @@
         (ft_ref.at[0], left.at[pl.ds(0, width)]),
     ]
     rest = [copy(src, dst, sems.at[n]) for n, (src, dst) in enumerate(rest)]
-    loads = Stream(get_cb + rest, 5)
+    loads = Stream(get_cb + rest, 8)
     outs = []
 
     def put(src, dst):

time: 124 us -> 125 us (level)
  no operation moved by 1% of the time
where the time goes in v4:
time: 125 us; the launch traced here: 124 us
  waiting for transfers between devices  57.2 us (46%)
  Pallas kernels  42.3 us (34%)
  starting transfers between devices  23.8 us (19%)
    all_to_all x3, waiting for transfers between devices, exchange(): lax.all_to_all(v, 'dom', split_axis=0, concat_axis=0, tiled=True, axis_in...  55.7 us
    all_to_all x3, starting transfers between devices, exchange(): lax.all_to_all(v, 'dom', split_axis=0, concat_axis=0, tiled=True, axis_in...  21.5 us
    pallas_call x1, Pallas kernels, combine(): pl.pallas_call(combine_kernel, grid=(dst_tiles,), out_shape=out_shape, in...  11.9 us
    pallas_call x1, Pallas kernels, layer(): pl.pallas_call(layer_kernel, out_shape=[jax.ShapeDtypeStruct((nodes, widt...  8.06 us
    pallas_call x1, Pallas kernels, boundary(): pl.pallas_call(boundary_kernel, out_shape=[jax.ShapeDtypeStruct((peers, s...  6.18 us
    pallas_call x1, Pallas kernels, feats_grad(): pl.pallas_call(feats_grad_kernel, grid=(nodes // block,), out_shape=jax.S...  4.95 us
    pallas_call x1, Pallas kernels, gather(): pl.pallas_call(gather_kernel, out_shape=jax.ShapeDtypeStruct((peers, slot...  4.47 us
    pallas_call x1, Pallas kernels, scatter(): pl.pallas_call(functools.partial(scatter_kernel, chunks=chunks), out_shap...  3.35 us
  transfers between devices with their start and end apart: 5, of which 4 were waited for; matrix products, arithmetic and copies ran while one was open for 0% of the time, Pallas kernels for 21%

profile of v4, /device:TPU:1, one launch (start us, length us, event | category | flops | bytes accessed | tf_op | source)
XLA Modules:
  0.0 124.1 jit_solution(10743218965440420908)
XLA Ops:
  0.6 4.5 %gather_rows.1 = bf16[128,16,512]{2,1,0:T(8,128)(2,1)} custom-call(s32[16,128]{1,0:T(8,128)} %bitcast.6, s32[1,128]{1,0:T(1,128)} %cnt_ref.5, bf16[1024,512]{1,0:T(8,128)(2,1)} %rows_ref.1), custom_call_target="tpu_custom_call" | custom-call | flops 2147483648 | bytes 3145728 | tf_op jit(solution)/shard_map/gather_rows/pallas_call | solution.py:103
  5.1 11.5 %all-to-all-start = ((bf16[128,16,512]{2,1,0:T(8,128)(2,1)}), bf16[128,16,512]{2,1,0:T(8,128)(2,1)S(1)}, u32[]{:S(2)}, u32[]{:S(2)}) async-start(bf16[128,16,512]{2,1,0:T(8,128)(2,1)} %gather_rows.1), calls=%async_computation | async-start | bytes 4194304 | tf_op jit(solution)/shard_map/all_to_all | solution.py:564
  16.6 11.9 %combine_tiles.1 = (bf16[1024,2048]{1,0:T(8,128)(2,1)}, bf16[2048,1024]{1,0:T(8,128)(2,1)}, bf16[1024,1024]{1,0:T(8,128)(2,1)}, f32[1024,512]{1,0:T(8,128)}, f32...) custom-call(s32[8,16]{1,0:T(8,128)} %src_ref.1, ...), custom_call_target="tpu_custom_call" | custom-call | flops 1610612736 | bytes 20971520 | tf_op jit(solution)/shard_map/combine_tiles/pallas_call | solution.py:178
  28.5 18.5 %all-to-all-done = bf16[128,16,512]{2,1,0:T(8,128)(2,1)S(1)} async-done(((bf16[128,16,512]{2,1,0:T(8,128)(2,1)}), bf16[128,16,512]{2,1,0:T(8,128)(2,1)S(1)}, u32[]{:S(2)}, u32[]{:S(2)}) %all-to-all-start) | async-done | bytes 2097184 | tf_op jit(solution)/shard_map/all_to_all | solution.py:564
  47.0 8.1 %layer.1 = (bf16[1024,512]{1,0:T(8,128)(2,1)}, bf16[16,1024,512]{2,1,0:T(8,128)(2,1)}, f32[64,2,16,128]{3,2,1,0:T(8,128)S(1)}, bf16[64,2,16,128]{3,2,1,0:T(8,128)(2,1)S(1)}) custom-call(bf16[1024,2048]{1,0:T(8,128)(2,1)} %get-tuple-element.24.cb_ref, bf16[2048,512]{1,0:T(8,128)(2,1)S(1)} %bitcast.3, f32[1024,512]{1,0:T(8,128)} %get-tuple-element.25.self_ref, ...), custom_call_target="tpu_custom_call" | custom-call | flops 3758096384 | bytes 18874368 | tf_op jit(solution)/shard_map/layer/pallas_call | solution.py:294
  55.1 1.2 collective-permute-start
  56.3 1.5 %collective-permute-done.got_ref = bf16[64,2,16,128]{3,2,1,0:T(8,128)(2,1)S(1)} collective-permute-done((bf16[64,2,16,128]{3,2,1,0:T(8,128)(2,1)S(1)}, bf16[64,2,16,128]{3,2,1,0:T(8,128)(2,1)S(1)}, u32[]{:S(2)}, u32[]{:S(2)}) %collective-permute-start) | collective-permute-done | bytes 524320 | tf_op jit(solution)/shard_map/ppermute | solution.py:577
  57.8 0.9 add_pair.1
  58.7 4.6 %all-to-all-start.1 = ((bf16[64,2,16,128]{3,2,1,0:T(8,128)(2,1)}), bf16[64,2,16,128]{3,2,1,0:T(8,128)(2,1)S(1)}, u32[]{:S(2)}, u32[]{:S(2)}) async-start(bf16[64,2,16,128]{3,2,1,0:T(8,128)(2,1)} %add_pair.1), calls=%async_computation.1 | async-start | bytes 1048576 | tf_op jit(solution)/shard_map/all_to_all | solution.py:564
  63.3 6.2 %boundary_grads.1 = (bf16[128,16,640]{2,1,0:T(8,128)(2,1)}, bf16[1024,512]{1,0:T(8,128)(2,1)}) custom-call(bf16[2048,1024]{1,0:T(8,128)(2,1)} %get-tuple-element.32.cbt_ref, bf16[16,1024,512]{2,1,0:T(8,128)(2,1)} %get-tuple-element.33.gpre_ref, bf16[512,512]{1,0:T(8,128)(2,1)} %get-tuple-element.34.wnt_ref), custom_call_target="tpu_custom_call" | custom-call | flops 2684354560 | bytes 9437184 | tf_op jit(solution)/shard_map/boundary_grads/pallas_call | solution.py:365
  69.5 6.0 %all-to-all-done.1.parts_ref = bf16[64,2,16,128]{3,2,1,0:T(8,128)(2,1)S(1)} async-done(((bf16[64,2,16,128]{3,2,1,0:T(8,128)(2,1)}), bf16[64,2,16,128]{3,2,1,0:T(8,128)(2,1)S(1)}, u32[]{:S(2)}, u32[]{:S(2)}) %all-to-all-start.1) | async-done | bytes 524320 | tf_op jit(solution)/shard_map/all_to_all | solution.py:564
  75.5 1.0 lay_shares.1
  76.5 5.4 %all-to-all-start.2 = ((bf16[128,16,640]{2,1,0:T(8,128)(2,1)}), bf16[128,16,640]{2,1,0:T(8,128)(2,1)S(1)}, u32[]{:S(2)}, u32[]{:S(2)}) async-start(bf16[128,16,640]{2,1,0:T(8,128)(2,1)} %lay_shares.1), calls=%async_computation.2 | async-start | bytes 5242880 | tf_op jit(solution)/shard_map/all_to_all | solution.py:564
  81.9 5.0 %feats_grad.1 = bf16[1024,512]{1,0:T(8,128)(2,1)} custom-call(bf16[1024,1024]{1,0:T(8,128)(2,1)} %get-tuple-element.36.cot_ref, bf16[1024,512]{1,0:T(8,128)(2,1)} %get-tuple-element.37.gagg_ref, bf16[16,1024,512]{2,1,0:T(8,128)(2,1)} %get-tuple-element.33.gpre_ref, bf16[512,512]{1,0:T(8,128)(2,1)} %get-tuple-element.38.wst_ref, bf16[1024,512]{1,0:T(8,128)(2,1)} %stale_ref.1), custom_call_target="tpu_custom_call" | custom-call | flops 1610612736 | bytes 7340032 | tf_op jit(solution)/shard_map/feats_grad/pallas_call | solution.py:398
  86.8 0.0 copy-start
  86.8 0.0 copy-start.1
  86.8 31.2 %all-to-all-done.2.ret_ref = bf16[128,16,640]{2,1,0:T(8,128)(2,1)S(1)} async-done(((bf16[128,16,640]{2,1,0:T(8,128)(2,1)}), bf16[128,16,640]{2,1,0:T(8,128)(2,1)S(1)}, u32[]{:S(2)}, u32[]{:S(2)}) %all-to-all-start.2) | async-done | bytes 2621472 | tf_op jit(solution)/shard_map/all_to_all | solution.py:564
  118.1 0.1 take_shares.1
  118.2 1.1 collective-permute-start.1
  119.3 0.0 copy-done
  119.3 0.0 copy-done.1
  119.3 3.4 %scatter_rows.1 = bf16[1024,512]{1,0:T(8,128)(2,1)} custom-call(s32[16,128]{1,0:T(8,128)S(1)} %bitcast.7, s32[1,128]{1,0:T(1,128)S(1)} %copy-done.1, bf16[128,16,640]{2,1,0:T(8,128)(2,1)S(1)} %all-to-all-done.2.ret_ref), custom_call_target="tpu_custom_call" | custom-call | flops 2684354560 | bytes 4194304 | tf_op jit(solution)/shard_map/scatter_rows/pallas_call | solution.py:507
  122.6 0.0 collective-permute-done.1.other_ref
  122.6 1.5 %lay_weights.1 = (f32[512,512]{1,0:T(8,128)}, f32[512,512]{1,0:T(8,128)}) custom-call(bf16[64,2,16,128]{3,2,1,0:T(8,128)(2,1)S(1)} %bitcast.5, bf16[64,2,16,128]{3,2,1,0:T(8,128)(2,1)S(1)} %collective-permute-done.1.other_ref), custom_call_target="tpu_custom_call" | custom-call | flops 524288 | bytes 3145728 | tf_op jit(solution)/shard_map/lay_weights/pallas_call | solution.py:531
Async XLA Ops:
  5.1 41.9 %all-to-all-start = ((bf16[128,16,512]{2,1,0:T(8,128)(2,1)}), bf16[128,16,512]{2,1,0:T(8,128)(2,1)S(1)}, u32[]{:S(2)}, u32[]{:S(2)}) async-start(bf16[128,16,512]{2,1,0:T(8,128)(2,1)} %gather_rows.1), calls=%async_computation | async-start | bytes 4194304 | tf_op jit(solution)/shard_map/all_to_all | solution.py:564
  55.1 2.7 %collective-permute-start = (bf16[64,2,16,128]{3,2,1,0:T(8,128)(2,1)S(1)}, bf16[64,2,16,128]{3,2,1,0:T(8,128)(2,1)S(1)}, u32[]{:S(2)}, u32[]{:S(2)}) collective-permute-start(bf16[64,2,16,128]{3,2,1,0:T(8,128)(2,1)S(1)} %get-tuple-element.31), channel_id=1, source_target_pairs={{0,1},{1,0},{2,3},{3,2},{4,5},{5,4},{6,7},{7,6},{8,9},{9,8},{10,11... | collective-permute-start | bytes 1572872 | tf_op jit(solution)/shard_map/ppermute | solution.py:577
  58.7 16.8 %all-to-all-start.1 = ((bf16[64,2,16,128]{3,2,1,0:T(8,128)(2,1)}), bf16[64,2,16,128]{3,2,1,0:T(8,128)(2,1)S(1)}, u32[]{:S(2)}, u32[]{:S(2)}) async-start(bf16[64,2,16,128]{3,2,1,0:T(8,128)(2,1)} %add_pair.1), calls=%async_computation.1 | async-start | bytes 1048576 | tf_op jit(solution)/shard_map/all_to_all | solution.py:564
  76.5 41.6 %all-to-all-start.2 = ((bf16[128,16,640]{2,1,0:T(8,128)(2,1)}), bf16[128,16,640]{2,1,0:T(8,128)(2,1)S(1)}, u32[]{:S(2)}, u32[]{:S(2)}) async-start(bf16[128,16,640]{2,1,0:T(8,128)(2,1)} %lay_shares.1), calls=%async_computation.2 | async-start | bytes 5242880 | tf_op jit(solution)/shard_map/all_to_all | solution.py:564
  86.8 32.5 %copy-start = (s32[128,16]{0,1:T(8,128)S(1)}, s32[128,16]{0,1:T(8,128)}, u32[]{:S(2)}) copy-start(s32[128,16]{0,1:T(8,128)} %param.20) | copy-start | bytes 24580
  86.8 32.5 %copy-start.1 = (s32[1,128]{1,0:T(1,128)S(1)}, s32[1,128]{1,0:T(1,128)}, u32[]{:S(2)}) copy-start(s32[1,128]{1,0:T(1,128)} %cnt_ref.5) | copy-start | bytes 1540
  118.2 4.5 %collective-permute-start.1 = (bf16[64,2,16,128]{3,2,1,0:T(8,128)(2,1)S(1)}, bf16[64,2,16,128]{3,2,1,0:T(8,128)(2,1)S(1)}, u32[]{:S(2)}, u32[]{:S(2)}) collective-permute-start(bf16[64,2,16,128]{3,2,1,0:T(8,128)(2,1)S(1)} %bitcast.4), channel_id=1, source_target_pairs={{0,1},{1,0},{2,3},{3,2},{4,5},{5,4},{6,7},{7,6},{8,9},{9,8},{10,11... | collective-permute-start | bytes 1572872 | tf_op jit(solution)/shard_map/ppermute | solution.py:585
